TPU v7x, 256 devices: a whole 4x4x8 slice. The times are simulated.
256 devices in a mesh: head: 8 (over y, x_hi), tile: 32 (over z, x_lo, core).
Axes of the slice: x: 4 (x_hi: 2, x_lo: 2; x = x_hi * 2 + x_lo), y: 4, z: 8, core: 2. Of those that a mesh axis runs over, the one named last changes fastest.
Arguments:
- query: bfloat16 [32, 384, 2048], P('tile', None, 'head'), may hold values from -6 to 6
- key: bfloat16 [32, 384, 2048], P('tile', None, 'head'), may hold values from -6 to 6
- value: bfloat16 [32, 384, 2048], P('tile', None, 'head'), may hold values from -6 to 6
- grad_out: bfloat16 [32, 384, 2048], P('tile', 'head'), may hold values from -384 to 384
- gain_q: float32 [128], replicated, may hold values from 0.25 to 1.75
- gain_k: float32 [128], replicated, may hold values from 0.25 to 1.75
- window: int32 [16, 6], P('head'), may hold values from -1 to 1, as said below
Outputs:
- grad_query: bfloat16 [32, 384, 2048], P('tile', None, 'head')
- grad_key: bfloat16 [32, 384, 2048], P('tile', None, 'head')
- grad_value: bfloat16 [32, 384, 2048], P('tile', None, 'head')
Inputs may be any that keep to these rules, and one draw needn't show every extreme that they name: `window`: columns 0, 2, 4 (lowest offsets along frames, rows, columns) are -1 or 0 and columns 1, 3, 5 (highest) are 0 or 1.
All inputs are finite; a program needn't handle non-finite values.
Results may differ from a plain program's by a relative error of at most 0.0092.
Values may be sent and summed in bfloat16 or wider, within the bound.
A program may use at most 128 MiB of HBM per device.

v0:
```python
import math

import jax
import jax.numpy as jnp
from jax import lax
from jax.sharding import PartitionSpec as P

HS = 128
TF = 4
TR = 2


def from_behind(value, axis, steps):
    count = lax.axis_size(axis)
    first, last = (max(0, -steps), min(count, count - steps))
    return lax.ppermute(value, axis, [(source, source + steps) for source in range(first, last)])


def normed(values_in, gain):
    floats = values_in.astype(jnp.float32)
    return floats * lax.rsqrt(jnp.mean(floats * floats, axis=-1, keepdims=True) + 1e-06) * gain


def norm_pullback(values_in, gain, cotangent):
    _, pull = jax.vjp(lambda inner: normed(inner, gain), values_in.astype(jnp.float32))
    return pull(cotangent)[0]


def guarded(any_live, compute, nothing):
    return lax.cond(any_live, compute, nothing, 0)


def window_grads(query_norm, cotangent, stacked, allowed, group):
    count = stacked.shape[1]
    rows = stacked.shape[2]
    heads_here = query_norm.shape[1]
    blocks = count // group
    scale = 1.0 / math.sqrt(HS)
    key_blocks = stacked[0].reshape(blocks, group * rows, heads_here, HS)
    value_blocks = stacked[1].reshape(blocks, group * rows, heads_here, HS)
    block_allowed = allowed.reshape(blocks, group, heads_here)
    row_allowed = jnp.swapaxes(jnp.repeat(block_allowed, rows, axis=1), 1, 2)
    block_live = jnp.any(block_allowed, axis=(1, 2))
    query_rows = query_norm.shape[0]

    def weights(key_block, value_block, live):
        scores = (
            jnp.einsum("qhd,khd->hqk", query_norm, key_block, preferred_element_type=jnp.float32)
            * scale
        )
        unnorm = jnp.where(live[:, None, :], jnp.exp(scores), 0.0)
        dprobs = jnp.einsum(
            "qhd,khd->hqk", cotangent, value_block, preferred_element_type=jnp.float32
        )
        return (unnorm, dprobs)

    def first_pass(carry, inputs):
        key_block, value_block, live, any_live = inputs

        def compute(unused):
            unnorm, dprobs = weights(key_block, value_block, live)
            return (jnp.sum(unnorm, axis=-1), jnp.sum(unnorm * dprobs, axis=-1))

        def nothing(unused):
            zeros = jnp.zeros((heads_here, query_rows), jnp.float32)
            return (zeros, zeros)

        terms = guarded(any_live, compute, nothing)
        return ((carry[0] + terms[0], carry[1] + terms[1]), None)

    start = jnp.zeros((heads_here, query_rows), jnp.float32)
    (totals, weighted), _ = lax.scan(
        first_pass, (start, start), (key_blocks, value_blocks, row_allowed, block_live)
    )
    centre = weighted / totals

    def second_pass(dquery, inputs):
        key_block, value_block, live, any_live = inputs

        def compute(unused):
            unnorm, dprobs = weights(key_block, value_block, live)
            probs = unnorm / totals[..., None]
            dscore = (probs * (dprobs - centre[..., None])).astype(jnp.bfloat16)
            probs_low = probs.astype(jnp.bfloat16)
            dquery_part = (
                jnp.einsum("hqk,khd->qhd", dscore, key_block, preferred_element_type=jnp.float32)
                * scale
            )
            dkey_part = (
                jnp.einsum("hqk,qhd->khd", dscore, query_norm, preferred_element_type=jnp.float32)
                * scale
            )
            dvalue_part = jnp.einsum(
                "hqk,qhd->khd", probs_low, cotangent, preferred_element_type=jnp.float32
            )
            return (dquery_part, dkey_part, dvalue_part)

        def nothing(unused):
            zeros_keys = jnp.zeros((group * rows, heads_here, HS), jnp.float32)
            return (jnp.zeros((query_rows, heads_here, HS), jnp.float32), zeros_keys, zeros_keys)

        dquery_part, dkey_part, dvalue_part = guarded(any_live, compute, nothing)
        return (dquery + dquery_part, (dkey_part, dvalue_part))

    dquery, (dkey_all, dvalue_all) = lax.scan(
        second_pass,
        jnp.zeros((query_rows, heads_here, HS), jnp.float32),
        (key_blocks, value_blocks, row_allowed, block_live),
    )
    parts = jnp.stack(
        [
            dkey_all.reshape(count, rows, heads_here * HS),
            dvalue_all.reshape(count, rows, heads_here * HS),
        ]
    )
    return (dquery, parts)


def widen(stacked, stride):
    pieces = []
    for offset in (stride, -stride):
        pieces.append(from_behind(stacked, "tile", offset))
    return jnp.concatenate([pieces[0], stacked, pieces[1]], axis=1)


def narrow(parts, stride):
    third = parts.shape[1] // 3
    lower = parts[:, :third]
    middle = parts[:, third : 2 * third]
    upper = parts[:, 2 * third :]
    for offset, piece in ((-stride, lower), (stride, upper)):
        middle = middle + from_behind(piece, "tile", offset)
    return middle


def widen_frames(stacked, stride):
    pieces = []
    for offset in (stride, -stride):
        pieces.append(from_behind(stacked, "tile", offset))
    return jnp.concatenate([pieces[0], stacked, pieces[1]], axis=1)


def narrow_frames(parts, stride):
    third = parts.shape[1] // 3
    lower = parts[:, :third]
    middle = parts[:, third : 2 * third]
    upper = parts[:, 2 * third :]
    for offset, piece in ((-stride, lower), (stride, upper)):
        middle = middle + from_behind(piece, "tile", offset)
    return middle


def shards(query, key, value, grad_out, gain_q, gain_k, window):
    rows = query.shape[1]
    features = query.shape[2]
    heads_here = features // HS
    relaid = lax.all_to_all(grad_out, "head", split_axis=2, concat_axis=1, tiled=True)
    query_heads = query[0].reshape(rows, heads_here, HS)
    key_heads = key[0].reshape(rows, heads_here, HS)
    cotangent = relaid[0].reshape(rows, heads_here, HS)
    query_norm = normed(query_heads, gain_q).astype(jnp.bfloat16)
    key_norm = normed(key_heads, gain_k).astype(jnp.bfloat16)
    key_value = jnp.stack([key_norm.reshape(rows, features), value[0]])[:, None]
    count = lax.axis_size("tile")
    across = count // (TF * TR)
    plane = TR * across
    own_index = lax.axis_index("tile")
    own_frame = own_index // plane
    own_row = own_index // across % TR
    own_col = own_index % across
    stacked = widen(key_value, 1)
    stacked = widen(stacked, across)
    stacked = widen_frames(stacked, plane)
    offsets = jnp.arange(27, dtype=jnp.int32)
    off_frame = offsets // 9 - 1
    off_row = offsets // 3 % 3 - 1
    off_col = offsets % 3 - 1
    inside = (own_frame + off_frame >= 0) & (own_frame + off_frame < TF)
    inside = inside & (own_row + off_row >= 0) & (own_row + off_row < TR)
    inside = inside & (own_col + off_col >= 0) & (own_col + off_col < across)
    allowed = (off_frame[:, None] >= window[None, :, 0]) & (
        off_frame[:, None] <= window[None, :, 1]
    )
    allowed = (
        allowed
        & (off_row[:, None] >= window[None, :, 2])
        & (off_row[:, None] <= window[None, :, 3])
    )
    allowed = (
        allowed
        & (off_col[:, None] >= window[None, :, 4])
        & (off_col[:, None] <= window[None, :, 5])
    )
    allowed = allowed & inside[:, None]
    dquery, parts = window_grads(query_norm, cotangent, stacked, allowed, 3)
    parts = narrow_frames(parts, plane)
    for stride in (across, 1):
        parts = narrow(parts, stride)
    summed = parts[:, 0]
    grad_query = (
        norm_pullback(query_heads, gain_q, dquery).astype(jnp.bfloat16).reshape(1, rows, features)
    )
    dkey_norm = summed[0].reshape(rows, heads_here, HS)
    grad_key = (
        norm_pullback(key_heads, gain_k, dkey_norm).astype(jnp.bfloat16).reshape(1, rows, features)
    )
    grad_value = summed[1].astype(jnp.bfloat16).reshape(1, rows, features)
    return (grad_query, grad_key, grad_value)


def solution(mesh):
    placed = (
        P("tile", None, "head"),
        P("tile", None, "head"),
        P("tile", None, "head"),
        P("tile", "head", None),
        P(),
        P(),
        P("head", None),
    )
    return jax.shard_map(
        shards,
        mesh=mesh,
        in_specs=placed,
        out_specs=(P("tile", None, "head"), P("tile", None, "head"), P("tile", None, "head")),
        check_vma=False,
    )
```

profile of v0, /device:TPU:1, one launch (start us, length us, event | category | flops | bytes accessed | tf_op | source)
XLA Modules:
  0.0 901.0 jit_solution(10764747321425351686)
XLA Ops:
  5.7 5.1 collective-permute-start.1
  15.6 4.4 collective-permute-done
  20.2 3.7 collective-permute-start.2
  25.2 24.3 %collective-permute-done.2 = bf16[2,3,384,256]{3,2,0,1:T(8,128)(2,1)S(1)} collective-permute-done((bf16[2,3,384,256]{3,2,0,1:T(8,128)(2,1)S(1)}, bf16[2,3,384,256]{3,2,0,1:T(8,128)(2,1)S(1)}, u32[]{:S(2)}, u32[]{:S(2)}) %collective-permute-start.2) | collective-permute-done | bytes 1179680 | tf_op jit(solution)/shard_map/ppermute | solution.py:16
  54.8 6.9 collective-permute-start.4
  65.5 12.6 %reduce.12 = bf16[2048,48]{1,0:T(8,128)(2,1)S(1)} reduce(bf16[2048,1,48]{2,1,0:T(2,128)(2,1)} %bitcast.108, bf16[]{:T(256)} %broadcast.476), dimensions={1}, to_apply=%bitcast.82.reduce_sub_computation | reduce | bytes 393218
  79.5 6.3 all-to-all-start
  93.3 3.5 reshape.289
  104.5 30.0 %collective-permute-done.4 = bf16[2,9,384,256]{3,2,0,1:T(8,128)(2,1)} collective-permute-done((bf16[2,9,384,256]{3,2,0,1:T(8,128)(2,1)}, bf16[2,9,384,256]{3,2,0,1:T(8,128)(2,1)}, u32[]{:S(2)}, u32[]{:S(2)}) %collective-permute-start.4) | collective-permute-done | bytes 3538976 | tf_op jit(solution)/shard_map/ppermute | solution.py:16
  134.4 4.1 constant_dynamic-update-slice_fusion.11
  143.1 73.1 %collective-permute-done.5 = bf16[2,9,384,256]{3,2,0,1:T(8,128)(2,1)} collective-permute-done((bf16[2,9,384,256]{3,2,0,1:T(8,128)(2,1)}, bf16[2,9,384,256]{3,2,0,1:T(8,128)(2,1)}, u32[]{:S(2)}, u32[]{:S(2)}) %collective-permute-start.5) | collective-permute-done | bytes 3538976 | tf_op jit(solution)/shard_map/ppermute | solution.py:16
  216.2 4.1 constant_dynamic-update-slice_fusion.5
  220.4 9.2 %fusion.57 = (bf16[1,27,384,256]{3,2,0,1:T(8,128)(2,1)}, bf16[1,27,384,256]{3,2,0,1:T(8,128)(2,1)}) fusion(bf16[2,27,384,256]{3,2,0,1:T(8,128)(2,1)} %constant_dynamic-update-slice_fusion.5), kind=kLoop, calls=%fused_computation.120 | loop fusion | bytes 21233664 | tf_op jit(solution)/shard_map/slice | solution.py:40
  229.6 10.8 %reshape_squeeze.17 = bf16[9,1152,2,128]{3,2,1,0:T(2,128)(2,1)} reshape(bf16[1,27,384,256]{3,2,0,1:T(8,128)(2,1)} %get-tuple-element.608) | data formatting | bytes 10616832 | tf_op jit(solution)/shard_map/reshape;squeeze | solution.py:40
  240.4 6.0 copy.116
  246.4 10.8 %reshape_squeeze.16 = bf16[9,1152,2,128]{3,2,1,0:T(2,128)(2,1)} reshape(bf16[1,27,384,256]{3,2,0,1:T(8,128)(2,1)} %get-tuple-element.609) | data formatting | bytes 10616832 | tf_op jit(solution)/shard_map/reshape;squeeze | solution.py:39
  257.2 6.0 copy.118
  263.2 34.7 %while.28 = (s32[]{:T(128)}, f32[2,384]{1,0:T(2,128)S(1)}, f32[2,384]{1,0:T(2,128)S(1)}, pred[9]{0:T(512)(128)(4,1)}, bf16[9,1152,2,128]{3,1,2,0:T(8,128)(2,1)},...) while((s32[]{:T(128)}, f32[2,384]{1,0:T(2,128)S(1)}, ...), condition=%wide.region_8.9_spmd.clone, body=%wide.region_3.8_spmd.clone.sunk | while | flops 457410048 | bytes 8787204 | solution.py:72
  273.8 3.9 conditional.6
  279.8 3.9 conditional.6
  287.9 3.9 conditional.6
  293.9 3.9 conditional.6
  297.9 111.0 %while.29 = (s32[]{:T(128)}, f32[384,2,128]{2,0,1:T(8,128)S(1)}, f32[9,1152,2,128]{3,2,1,0:T(2,128)}, f32[9,1152,2,128]{3,2,1,0:T(2,128)}, pred[9]{0:T(512)(128)...) while((s32[]{:T(128)}, f32[384,2,128]{2,0,1:T(8,128)S(1)}, ...), condition=%wide.region_12.13_spmd.clone, body=%wide.region_9.12_spmd.clone.sunk | while | flops 1139245056 | bytes 27250992 | solution.py:105
  301.1 5.9 copy_dynamic-update-slice_fusion.3
  310.0 5.9 copy_dynamic-update-slice_fusion.3
  319.0 5.9 copy_dynamic-update-slice_fusion.3
  327.9 5.9 copy_dynamic-update-slice_fusion.3
  336.5 7.8 conditional.7
  344.4 6.0 copy_dynamic-update-slice_fusion.3
  353.0 7.8 conditional.7
  361.0 5.9 copy_dynamic-update-slice_fusion.3
  369.9 6.0 copy_dynamic-update-slice_fusion.3
  378.5 7.8 conditional.7
  386.5 6.0 copy_dynamic-update-slice_fusion.3
  395.1 7.8 conditional.7
  403.0 5.9 copy_dynamic-update-slice_fusion.3
  409.0 14.1 %stack_reshape.8 = f32[1,27,384,256]{3,2,1,0:T(8,128)} reshape(f32[9,1152,2,128]{3,2,1,0:T(2,128)} %get-tuple-element.258) | data formatting | bytes 21233664 | tf_op jit(solution)/shard_map/stack;reshape | solution.py:110
  423.1 14.2 %stack_reshape.7 = f32[1,27,384,256]{3,2,1,0:T(8,128)} reshape(f32[9,1152,2,128]{3,2,1,0:T(2,128)} %get-tuple-element.257) | data formatting | bytes 21233664 | tf_op jit(solution)/shard_map/stack;reshape | solution.py:110
  437.3 9.7 %constant_dynamic-update-slice_fusion.13 = f32[2,27,384,256]{3,2,1,0:T(8,128)} fusion(f32[1,27,384,256]{3,2,1,0:T(8,128)} %stack_reshape.7), kind=kLoop, calls=%fused_computation.85 | loop fusion | bytes 21233664
  447.0 4.8 constant_dynamic-update-slice_fusion.12
  451.8 11.5 %fusion.56 = (f32[2,9,384,256]{3,2,1,0:T(8,128)}, f32[2,9,384,256]{3,2,1,0:T(8,128)}) fusion(f32[2,27,384,256]{3,2,1,0:T(8,128)} %constant_dynamic-update-slice_fusion.12), kind=kLoop, calls=%fused_computation.119 | loop fusion | bytes 28311552 | tf_op jit(solution)/shard_map/slice | solution.py:145
  464.6 32.9 %collective-permute-start.7 = (f32[2,9,384,256]{3,2,1,0:T(8,128)}, f32[2,9,384,256]{3,2,1,0:T(8,128)}, u32[]{:S(2)}, u32[]{:S(2)}) collective-permute-start(f32[2,9,384,256]{3,2,1,0:T(8,128)} %get-tuple-element.607), channel_id=1, source_target_pairs={{0,8},{1,9},{2,10},{3,11},{4,12},{5,13},{6,14},{7,15},{8,16},{9,17... | collective-permute-start | bytes 21233672 | tf_op jit(solution)/shard_map/ppermute | solution.py:16
  497.5 294.5 %collective-permute-done.6 = f32[2,9,384,256]{3,2,1,0:T(8,128)} collective-permute-done((f32[2,9,384,256]{3,2,1,0:T(8,128)}, f32[2,9,384,256]{3,2,1,0:T(8,128)}, u32[]{:S(2)}, u32[]{:S(2)}) %collective-permute-start.6) | collective-permute-done | bytes 7077920 | tf_op jit(solution)/shard_map/ppermute | solution.py:16
  792.0 11.5 %fusion.32 = f32[2,9,384,256]{3,2,1,0:T(8,128)} fusion(f32[2,9,384,256]{3,2,1,0:T(8,128)} %collective-permute-done.7, f32[2,9,384,256]{3,2,1,0:T(8,128)} %collective-permute-done.6, f32[2,27,384,256]{3,2,1,0:T(8,128)} %constant_dynamic-update-slice_fusion.12), kind=kLoop, calls=%fused_computation.45 | loop fusion | flops 3538944 | bytes 28311552 | tf_op jit(solution)/shard_map/add | solution.py:149
  807.5 11.2 %collective-permute-start.9 = (f32[2,3,384,256]{3,2,1,0:T(8,128)S(1)}, f32[2,3,384,256]{3,2,1,0:T(8,128)S(1)}, u32[]{:S(2)}, u32[]{:S(2)}) collective-permute-start(f32[2,3,384,256]{3,2,1,0:T(8,128)S(1)} %get-tuple-element.611), channel_id=1, source_target_pairs={{0,4},{1,5},{2,6},{3,7},{4,8},{5,9},{6,10},{7,11},{8,12},{9,13},{1... | collective-permute-start | bytes 7077896 | tf_op jit(solution)/shard_map/ppermute | solution.py:16
  818.7 49.1 %collective-permute-done.8 = f32[2,3,384,256]{3,2,1,0:T(8,128)S(1)} collective-permute-done((f32[2,3,384,256]{3,2,1,0:T(8,128)S(1)}, f32[2,3,384,256]{3,2,1,0:T(8,128)S(1)}, u32[]{:S(2)}, u32[]{:S(2)}) %collective-permute-start.8) | collective-permute-done | bytes 2359328 | tf_op jit(solution)/shard_map/ppermute | solution.py:16
  879.1 6.7 collective-permute-done.10
  885.8 9.4 %collective-permute-done.11 = f32[2,1,384,256]{3,2,1,0:T(8,128)} collective-permute-done((f32[2,1,384,256]{3,2,1,0:T(8,128)}, f32[2,1,384,256]{3,2,1,0:T(8,128)}, u32[]{:S(2)}, u32[]{:S(2)}) %collective-permute-start.11) | collective-permute-done | bytes 786464 | tf_op jit(solution)/shard_map/ppermute | solution.py:16
  (278 shorter events, 143.8 us)
Async XLA Ops:
  0.6 5.0 copy-start.10
  1.3 18.8 %copy-start.22 = (f32[256]{0:T(256)}, f32[256]{0:T(256)S(1)}, u32[]{:S(2)}) copy-start(f32[256]{0:T(256)S(1)} %broadcast_bitcast_fusion) | copy-start | bytes 3076
  2.5 17.7 %copy-start.3 = (f32[384,2,128]{2,1,0:T(2,128)}, f32[384,2,128]{2,1,0:T(2,128)S(1)}, u32[]{:S(2)}) copy-start(f32[384,2,128]{2,1,0:T(2,128)S(1)} %reshape.270) | copy-start | bytes 1179652
  3.0 0.6 copy-start.16
  4.5 15.7 %copy-start.7 = (f32[1,384,256]{2,1,0:T(8,128)}, f32[1,384,256]{2,1,0:T(8,128)S(1)}, u32[]{:S(2)}) copy-start(f32[1,384,256]{2,1,0:T(8,128)S(1)} %mul.185) | copy-start | bytes 1179652
  5.6 46.6 %copy-start.8 = (bf16[1,384,256]{2,1,0:T(8,128)(2,1)}, bf16[1,384,256]{2,1,0:T(8,128)(2,1)S(1)}, u32[]{:S(2)}) copy-start(bf16[1,384,256]{2,1,0:T(8,128)(2,1)S(1)} %multiply_convert_fusion) | copy-start | bytes 589828
  5.7 10.0 %collective-permute-start.1 = (bf16[2,1,384,256]{3,2,0,1:T(8,128)(2,1)S(1)}, bf16[2,1,384,256]{3,2,0,1:T(8,128)(2,1)S(1)}, u32[]{:S(2)}, u32[]{:S(2)}) collective-permute-start(bf16[2,1,384,256]{3,2,0,1:T(8,128)(2,1)S(1)} %maximum_bitcast_fusion), channel_id=1, source_target_pairs={{1,0},{2,1},{3,2},{4,3},{5,4},{6,5},{7,6},{8,7},{9,8},{10,9},{11,1... | collective-permute-start | bytes 1179656 | tf_op jit(solution)/shard_map/ppermute | solution.py:16
  10.8 9.2 %collective-permute-start = (bf16[2,1,384,256]{3,2,0,1:T(8,128)(2,1)S(1)}, bf16[2,1,384,256]{3,2,0,1:T(8,128)(2,1)S(1)}, u32[]{:S(2)}, u32[]{:S(2)}) collective-permute-start(bf16[2,1,384,256]{3,2,0,1:T(8,128)(2,1)S(1)} %maximum_bitcast_fusion), channel_id=1, source_target_pairs={{0,1},{1,2},{2,3},{3,4},{4,5},{5,6},{6,7},{7,8},{8,9},{9,10},{10,1... | collective-permute-start | bytes 1179656 | tf_op jit(solution)/shard_map/ppermute | solution.py:16
  20.0 32.9 %copy-start.5 = (bf16[2,1,384,256]{3,2,0,1:T(8,128)(2,1)}, bf16[2,1,384,256]{3,2,0,1:T(8,128)(2,1)S(1)}, u32[]{:S(2)}) copy-start(bf16[2,1,384,256]{3,2,0,1:T(8,128)(2,1)S(1)} %collective-permute-done) | copy-start | bytes 1179652
  20.2 42.9 %copy-start.12 = (bf16[1,48,2048]{2,1,0:T(8,128)(2,1)S(1)}, bf16[1,48,2048]{2,1,0:T(8,128)(2,1)}, u32[]{:S(2)}) copy-start(bf16[1,48,2048]{2,1,0:T(8,128)(2,1)} %param.18) | copy-start | bytes 589828
  20.2 29.3 %collective-permute-start.2 = (bf16[2,3,384,256]{3,2,0,1:T(8,128)(2,1)S(1)}, bf16[2,3,384,256]{3,2,0,1:T(8,128)(2,1)S(1)}, u32[]{:S(2)}, u32[]{:S(2)}) collective-permute-start(bf16[2,3,384,256]{3,2,0,1:T(8,128)(2,1)S(1)} %pad_maximum_fusion), channel_id=1, source_target_pairs={{0,4},{1,5},{2,6},{3,7},{4,8},{5,9},{6,10},{7,11},{8,12},{9,13},{1... | collective-permute-start | bytes 3538952 | tf_op jit(solution)/shard_map/ppermute | solution.py:16
  23.9 29.7 %collective-permute-start.3 = (bf16[2,3,384,256]{3,2,0,1:T(8,128)(2,1)S(1)}, bf16[2,3,384,256]{3,2,0,1:T(8,128)(2,1)S(1)}, u32[]{:S(2)}, u32[]{:S(2)}) collective-permute-start(bf16[2,3,384,256]{3,2,0,1:T(8,128)(2,1)S(1)} %pad_maximum_fusion), channel_id=1, source_target_pairs={{4,0},{5,1},{6,2},{7,3},{8,4},{9,5},{10,6},{11,7},{12,8},{13,9},{1... | collective-permute-start | bytes 3538952 | tf_op jit(solution)/shard_map/ppermute | solution.py:16
  52.9 34.8 %copy-start.20 = (f32[128]{0:T(128)S(1)}, f32[128]{0:T(128)}, u32[]{:S(2)}) copy-start(f32[128]{0:T(128)} %param.19) | copy-start | bytes 1540
  52.9 36.7 %copy-start.13 = (s32[2,6]{1,0:T(2,128)S(1)}, s32[2,6]{1,0:T(2,128)}, u32[]{:S(2)}) copy-start(s32[2,6]{1,0:T(2,128)} %param.21) | copy-start | bytes 148
  54.8 79.7 %collective-permute-start.4 = (bf16[2,9,384,256]{3,2,0,1:T(8,128)(2,1)}, bf16[2,9,384,256]{3,2,0,1:T(8,128)(2,1)}, u32[]{:S(2)}, u32[]{:S(2)}) collective-permute-start(bf16[2,9,384,256]{3,2,0,1:T(8,128)(2,1)} %constant_dynamic-update-slice_fusion), channel_id=1, source_target_pairs={{0,8},{1,9},{2,10},{3,11},{4,12},{5,13},{6,14},{7,15},{8,16},{9,17... | collective-permute-start | bytes 10616840 | tf_op jit(solution)/shard_map/ppermute | solution.py:16
  61.7 154.5 %collective-permute-start.5 = (bf16[2,9,384,256]{3,2,0,1:T(8,128)(2,1)}, bf16[2,9,384,256]{3,2,0,1:T(8,128)(2,1)}, u32[]{:S(2)}, u32[]{:S(2)}) collective-permute-start(bf16[2,9,384,256]{3,2,0,1:T(8,128)(2,1)} %constant_dynamic-update-slice_fusion), channel_id=1, source_target_pairs={{8,0},{9,1},{10,2},{11,3},{12,4},{13,5},{14,6},{15,7},{16,8},{17,9... | collective-permute-start | bytes 10616840 | tf_op jit(solution)/shard_map/ppermute | solution.py:16
  79.5 13.8 %all-to-all-start = ((bf16[8,2,6144]{2,1,0:T(2,128)(2,1)}), bf16[8,2,6144]{2,1,0:T(2,128)(2,1)}, u32[]{:S(2)}, u32[]{:S(2)}) async-start(bf16[8,2,6144]{2,1,0:T(2,128)(2,1)} %reshape.288), calls=%async_computation | async-start | bytes 393216 | tf_op jit(solution)/shard_map/all_to_all | solution.py:157
  87.0 14.8 %copy-start.1 = (bf16[1,384,256]{1,2,0:T(8,128)(2,1)}, bf16[1,384,256]{1,2,0:T(8,128)(2,1)S(1)}, u32[]{:S(2)}) copy-start(bf16[1,384,256]{1,2,0:T(8,128)(2,1)S(1)} %copy.110) | copy-start | bytes 589828
  87.1 0.6 copy-start.18
  87.7 50.8 %copy-start.14 = (f32[384,2]{0,1:T(2,128)}, f32[384,2]{0,1:T(2,128)S(1)}, u32[]{:S(2)}) copy-start(f32[384,2]{0,1:T(2,128)S(1)} %fusion.53) | copy-start | bytes 9220
  104.5 35.2 %copy-start.6 = (bf16[2,1,384,256]{3,2,0,1:T(8,128)(2,1)S(1)}, bf16[2,1,384,256]{3,2,0,1:T(8,128)(2,1)}, u32[]{:S(2)}) copy-start(bf16[2,1,384,256]{3,2,0,1:T(8,128)(2,1)} %copy-done.5) | copy-start | bytes 1179652
  104.5 36.0 %copy-start.9 = (bf16[1,384,256]{2,1,0:T(8,128)(2,1)S(1)}, bf16[1,384,256]{2,1,0:T(8,128)(2,1)}, u32[]{:S(2)}) copy-start(bf16[1,384,256]{2,1,0:T(8,128)(2,1)} %copy-done.8) | copy-start | bytes 589828
  104.5 36.0 %copy-start.11 = (bf16[1,384,256]{2,1,0:T(8,128)(2,1)S(1)}, bf16[1,384,256]{2,1,0:T(8,128)(2,1)}, u32[]{:S(2)}) copy-start(bf16[1,384,256]{2,1,0:T(8,128)(2,1)} %param.17) | copy-start | bytes 589828
  437.3 9.7 %copy-start = (f32[1,27,384,256]{3,2,1,0:T(8,128)S(1)}, f32[1,27,384,256]{3,2,1,0:T(8,128)}, u32[]{:S(2)}) copy-start(f32[1,27,384,256]{3,2,1,0:T(8,128)} %stack_reshape.8) | copy-start | bytes 31850500
  463.3 328.7 %collective-permute-start.6 = (f32[2,9,384,256]{3,2,1,0:T(8,128)}, f32[2,9,384,256]{3,2,1,0:T(8,128)}, u32[]{:S(2)}, u32[]{:S(2)}) collective-permute-start(f32[2,9,384,256]{3,2,1,0:T(8,128)} %get-tuple-element.606), channel_id=1, source_target_pairs={{8,0},{9,1},{10,2},{11,3},{12,4},{13,5},{14,6},{15,7},{16,8},{17,9... | collective-permute-start | bytes 21233672 | tf_op jit(solution)/shard_map/ppermute | solution.py:16
  464.6 327.4 %collective-permute-start.7 = (f32[2,9,384,256]{3,2,1,0:T(8,128)}, f32[2,9,384,256]{3,2,1,0:T(8,128)}, u32[]{:S(2)}, u32[]{:S(2)}) collective-permute-start(f32[2,9,384,256]{3,2,1,0:T(8,128)} %get-tuple-element.607), channel_id=1, source_target_pairs={{0,8},{1,9},{2,10},{3,11},{4,12},{5,13},{6,14},{7,15},{8,16},{9,17... | collective-permute-start | bytes 21233672 | tf_op jit(solution)/shard_map/ppermute | solution.py:16
  806.2 61.7 %collective-permute-start.8 = (f32[2,3,384,256]{3,2,1,0:T(8,128)S(1)}, f32[2,3,384,256]{3,2,1,0:T(8,128)S(1)}, u32[]{:S(2)}, u32[]{:S(2)}) collective-permute-start(f32[2,3,384,256]{3,2,1,0:T(8,128)S(1)} %get-tuple-element.610), channel_id=1, source_target_pairs={{4,0},{5,1},{6,2},{7,3},{8,4},{9,5},{10,6},{11,7},{12,8},{13,9},{1... | collective-permute-start | bytes 7077896 | tf_op jit(solution)/shard_map/ppermute | solution.py:16
  807.5 61.2 %collective-permute-start.9 = (f32[2,3,384,256]{3,2,1,0:T(8,128)S(1)}, f32[2,3,384,256]{3,2,1,0:T(8,128)S(1)}, u32[]{:S(2)}, u32[]{:S(2)}) collective-permute-start(f32[2,3,384,256]{3,2,1,0:T(8,128)S(1)} %get-tuple-element.611), channel_id=1, source_target_pairs={{0,4},{1,5},{2,6},{3,7},{4,8},{5,9},{6,10},{7,11},{8,12},{9,13},{1... | collective-permute-start | bytes 7077896 | tf_op jit(solution)/shard_map/ppermute | solution.py:16
  870.9 7.0 copy-start.2
  870.9 7.0 copy-start.21
  870.9 7.2 copy-start.19
  870.9 7.2 copy-start.15
  872.2 13.6 %collective-permute-start.10 = (f32[2,1,384,256]{3,2,1,0:T(8,128)}, f32[2,1,384,256]{3,2,1,0:T(8,128)}, u32[]{:S(2)}, u32[]{:S(2)}) collective-permute-start(f32[2,1,384,256]{3,2,1,0:T(8,128)} %get-tuple-element.612), channel_id=1, source_target_pairs={{1,0},{2,1},{3,2},{4,3},{5,4},{6,5},{7,6},{8,7},{9,8},{10,9},{11,1... | collective-permute-start | bytes 2359304 | tf_op jit(solution)/shard_map/ppermute | solution.py:16
  875.4 19.8 %collective-permute-start.11 = (f32[2,1,384,256]{3,2,1,0:T(8,128)}, f32[2,1,384,256]{3,2,1,0:T(8,128)}, u32[]{:S(2)}, u32[]{:S(2)}) collective-permute-start(f32[2,1,384,256]{3,2,1,0:T(8,128)} %get-tuple-element.613), channel_id=1, source_target_pairs={{0,1},{1,2},{2,3},{3,4},{4,5},{5,6},{6,7},{7,8},{8,9},{9,10},{10,1... | collective-permute-start | bytes 2359304 | tf_op jit(solution)/shard_map/ppermute | solution.py:16
  877.9 19.7 %copy-start.4 = (f32[384,2,128]{2,1,0:T(2,128)S(1)}, f32[384,2,128]{2,1,0:T(2,128)}, u32[]{:S(2)}) copy-start(f32[384,2,128]{2,1,0:T(2,128)} %copy-done.3) | copy-start | bytes 1179652
  877.9 19.7 %copy-start.24 = (f32[128]{0:T(128)S(1)}, f32[128]{0:T(128)}, u32[]{:S(2)}) copy-start(f32[128]{0:T(128)} %param.20) | copy-start | bytes 1540
  878.3 19.9 %copy-start.17 = (f32[384,2]{0,1:T(2,128)S(1)}, f32[384,2]{0,1:T(2,128)}, u32[]{:S(2)}) copy-start(f32[384,2]{0,1:T(2,128)} %copy-done.16) | copy-start | bytes 9220
  879.1 20.1 %copy-start.23 = (f32[256]{0:T(256)S(1)}, f32[256]{0:T(256)}, u32[]{:S(2)}) copy-start(f32[256]{0:T(256)} %copy-done.22) | copy-start | bytes 3076
where the time goes:
time: 907 us; the launch traced here: 901 us
  waiting for transfers between devices  498 us (55%)
  local copies, waits for them, and re-layouts  230 us (25%)
  starting transfers between devices  78.9 us (9%)
  matrix products  43 us (5%)
  other arithmetic  36.6 us (4%)
  loops' own time  13.2 us (1%)
    ppermute x12, waiting for transfers between devices, from_behind(): lax.ppermute(value, axis, [(source, source + steps) for source in range(f...  496 us
    ppermute x12, starting transfers between devices, from_behind(): lax.ppermute(value, axis, [(source, source + steps) for source in range(f...  72.6 us
    dynamic_update_slice x9, local copies, waits for them, and re-layouts, window_grads(): lax.scan(second_pass, jnp.zeros((query_rows, heads_here, HS), jnp.float32...  53.5 us
    unnamed x70, local copies, waits for them, and re-layouts  45.6 us
    another operation x3, local copies, waits for them, and re-layouts, window_grads(): jnp.stack([dkey_all.reshape(count, rows, heads_here * HS), dvalue_all.res...  33.1 us
    dynamic_slice x18, local copies, waits for them, and re-layouts, window_grads(): lax.scan(first_pass, (start, start), (key_blocks, value_blocks, row_allow...  22.5 us
  transfers between devices with their start and end apart: 13, of which 12 were waited for; matrix products, arithmetic and copies ran while one was open for 5% of the time, Pallas kernels for 0%

commit v1 on v0

v1 whole, which is shorter than its diff:
```python
import math

import jax
import jax.numpy as jnp
from jax import lax
from jax.experimental import pallas as pl
from jax.experimental.pallas import tpu as pltpu
from jax.sharding import PartitionSpec as P

MESH = pl.DeviceIdType.MESH
HS = 128
TF, TR, TC = 4, 2, 4
ROWS = 384
PIECE = 48
GROUP = 8
PLANE = TR * TC
SCALE = 1.0 / math.sqrt(HS)
LOG2E = math.log2(math.e)
EXP_SCALE = SCALE * LOG2E
HIDE = 1e30
EPS = 1e-6

A2A = 0
KVROW = 8
KVCOL = 9
QF = 13
DOF = 15
PART = 17
TOTAL = 19
GCOL = 21
GROW = 25
GQ = 26
COPIES = 28


def dot(a, b):
    return jnp.dot(a, b, preferred_element_type=jnp.float32)


def fold8(x):
    return jnp.sum(x.reshape(x.shape[0] // 8, 8, x.shape[1]), axis=0)


def inv_rms(x):
    return lax.rsqrt(jnp.mean(x * x, axis=-1, keepdims=True) + EPS)


def pullback(x, gain, cotangent):
    rs = inv_rms(x)
    scaled = cotangent * gain
    along = jnp.mean(scaled * x, axis=-1, keepdims=True)
    return rs * scaled - x * (rs * rs * rs * along)


def kernel(
    window, q_ref, k_ref, v_ref, g_ref, gain_q, gain_k,
    gq_out, gk_out, gv_out,
    kv, qd, qdt, ktr, acc, dqt, part, part_in, total,
    col_out, col_in, row_out, row_in, dq_out, dq_in,
    ssem, rsem, lsem,
):
    me = lax.axis_index("head")
    tile = lax.axis_index("tile")
    frame = tile // PLANE
    row = tile // TC % TR
    col = tile % TC
    has_prev, has_next = frame > 0, frame < TF - 1
    has_left, has_right = col > 0, col < TC - 1
    partner = tile + TC * (1 - 2 * row)

    frame_to = (tile + PLANE, tile - PLANE)
    frame_sends = (has_next, has_prev)
    frame_gets = (has_prev, has_next)
    col_to = (tile + 1, tile - 1)
    col_sends = (has_right, has_left)
    col_gets = (has_left, has_right)

    started = []

    def remote(head, index, src, dst, axis, device):
        return pltpu.make_async_remote_copy(
            src_ref=src,
            dst_ref=dst,
            send_sem=ssem.at[head, index],
            recv_sem=rsem.at[head, index],
            device_id={axis: device},
            device_id_type=MESH,
        )

    def under(cond, fn):
        if cond is None:
            fn()
        else:
            pl.when(cond)(fn)

    def send(head, index, src, dst, device, cond=None):
        under(cond, lambda: remote(head, index, src, dst, "tile", device).start())
        started.append((cond, lambda: remote(head, index, src, dst, "tile", device).wait_send()))

    def arrive(head, index, dst, cond=None):
        under(cond, lambda: remote(head, index, dst, dst, "tile", partner).wait_recv())

    barrier = pltpu.get_barrier_semaphore()

    def greet(axis, device):
        pl.semaphore_signal(barrier, inc=1, device_id={axis: device}, device_id_type=MESH)

    for step in range(1, GROUP):
        greet("head", lax.rem(me + step, GROUP))
    greet("tile", partner)
    for slot in range(2):
        under(frame_sends[slot], lambda slot=slot: greet("tile", frame_to[slot]))
        under(col_sends[slot], lambda slot=slot: greet("tile", col_to[slot]))

    for head in range(2):
        lanes = pl.ds(head * HS, HS)
        x = k_ref[0, :, lanes].astype(jnp.float32)
        kv[head, 0, 1, 0] = (x * inv_rms(x) * gain_k[...]).astype(jnp.bfloat16)
        kv[head, 0, 1, 1] = v_ref[0, :, lanes]
        x = q_ref[0, :, lanes].astype(jnp.float32)
        qd[head, 1, 0] = (x * inv_rms(x) * gain_q[...]).astype(jnp.bfloat16)

    def clear(ref):
        ref[...] = jnp.zeros(ref.shape, ref.dtype)

    for slot in range(2):
        def no_frame(slot=slot):
            for head in range(2):
                clear(qd.at[head, 2 * slot])
                clear(part_in.at[head, slot])
                clear(total.at[head, 2 * slot])
                clear(dq_in.at[head, slot])

        def no_col(slot=slot):
            for head in range(2):
                for rr in range(2):
                    clear(kv.at[head, rr, 2 * slot])
                    clear(col_in.at[head, rr, slot])

        pl.when(jnp.logical_not(frame_gets[slot]))(no_frame)
        pl.when(jnp.logical_not(col_gets[slot]))(no_col)

    greeted = GROUP - 1 + 1
    for cond in (has_prev, has_next, has_left, has_right):
        greeted = greeted + jnp.where(cond, 1, 0)
    pl.semaphore_wait(barrier, greeted)

    def a2a(head, step):
        to = lax.rem(me + step, GROUP)
        src = g_ref.at[0, :, pl.ds(pl.multiple_of(to * (2 * HS) + head * HS, HS), HS)]
        dst = qd.at[head, 1, 1, pl.ds(pl.multiple_of(me * PIECE, 16), PIECE), :]
        return remote(head, A2A + step, src, dst, "head", to)

    def own_piece(head):
        src = g_ref.at[0, :, pl.ds(pl.multiple_of(me * (2 * HS) + head * HS, HS), HS)]
        dst = qd.at[head, 1, 1, pl.ds(pl.multiple_of(me * PIECE, 16), PIECE), :]
        return pltpu.make_async_copy(src, dst, lsem.at[head])

    def start_a2a(head):
        for step in range(1, GROUP):
            a2a(head, step).start()
            started.append((None, lambda step=step: a2a(head, step).wait_send()))
        own_piece(head).start()

    def end_a2a(head):
        for step in range(1, GROUP):
            come = lax.rem(me + GROUP - step, GROUP)
            dst = qd.at[head, 1, 1, pl.ds(pl.multiple_of(come * PIECE, 16), PIECE), :]
            remote(head, A2A + step, dst, dst, "head", come).wait_recv()
        own_piece(head).wait()

    def kv_row(head):
        send(head, KVROW, kv.at[head, 0, 1], kv.at[head, 1, 1], partner)

    def kv_cols(head, rr):
        for slot in range(2):
            send(
                head, KVCOL + 2 * rr + slot, kv.at[head, rr, 1], kv.at[head, rr, 2 * slot],
                col_to[slot], col_sends[slot],
            )

    def frames(head, base, kind):
        for slot in range(2):
            send(
                head, base + slot, qd.at[head, 1, kind], qd.at[head, 2 * slot, kind],
                frame_to[slot], frame_sends[slot],
            )

    def gather_first(head):
        kv_row(head)
        kv_cols(head, 0)
        frames(head, QF, 0)

    def gather_second(head):
        end_a2a(head)
        frames(head, DOF, 1)
        arrive(head, KVROW, kv.at[head, 1, 1])
        kv_cols(head, 1)

    def gather_end(head):
        for slot in range(2):
            arrive(head, QF + slot, qd.at[head, 2 * slot, 0], frame_gets[slot])
            arrive(head, DOF + slot, qd.at[head, 2 * slot, 1], frame_gets[slot])
            for rr in range(2):
                arrive(head, KVCOL + 2 * rr + slot, kv.at[head, rr, 2 * slot], col_gets[slot])

    def one_if(cond):
        return jnp.where(cond, 1, 0)

    def frame_mask(head, ff):
        if ff == 1:
            return 1
        if ff == 0:
            return window[head, 1] * one_if(has_prev)
        return -window[head, 0] * one_if(has_next)

    def row_mask(head, rr):
        other = jnp.where(row == 0, window[head, 3], -window[head, 2])
        return jnp.where(rr == 0, 1, other)

    def col_mask(head, cc):
        left = -window[head, 4] * one_if(has_left)
        right = window[head, 5] * one_if(has_right)
        return jnp.where(cc == 0, left, jnp.where(cc == 2, right, 1))

    def first_pass(head):
        for ff in range(3):
            for kind in range(2):
                qdt[head, ff, kind] = qd[head, ff, kind].T

        def body(i, carry):
            rr, cc = i // 3, i % 3
            keys, values = kv[head, rr, cc, 0], kv[head, rr, cc, 1]
            ktr[head, rr, cc] = keys.T
            place = row_mask(head, rr) * col_mask(head, cc)
            out = []
            for ff in range(3):
                live = jnp.where(place * frame_mask(head, ff) == 1, 1.0, 0.0)
                unnorm = jnp.exp2(dot(keys, qdt[head, ff, 0]) * EXP_SCALE)
                dprobs = dot(values, qdt[head, ff, 1])
                out.append(carry[2 * ff] + fold8(unnorm) * live)
                out.append(carry[2 * ff + 1] + fold8(unnorm * dprobs) * live)
            return tuple(out)

        zero = jnp.zeros((8, ROWS), jnp.float32)
        sums = lax.fori_loop(0, 6, body, (zero,) * 6)
        for ff in range(3):
            for at in range(2):
                part[head, ff, at : at + 1] = jnp.sum(sums[2 * ff + at], axis=0, keepdims=True)
            part[head, ff, 2:8] = jnp.zeros((6, ROWS), jnp.float32)

    def send_parts(head):
        for slot in range(2):
            send(
                head, PART + slot, part.at[head, 2 - 2 * slot], part_in.at[head, slot],
                frame_to[slot], frame_sends[slot],
            )

    def totals(head):
        for slot in range(2):
            arrive(head, PART + slot, part_in.at[head, slot], frame_gets[slot])
        both = part[head, 1, 0:2] + part_in[head, 0, 0:2] + part_in[head, 1, 0:2]
        total[head, 1, 0:1] = jnp.log(both[0:1]) * LOG2E
        total[head, 1, 1:2] = both[1:2] / both[0:1]
        total[head, 1, 2:8] = jnp.zeros((6, ROWS), jnp.float32)
        for slot in range(2):
            send(
                head, TOTAL + slot, total.at[head, 1], total.at[head, 2 * slot],
                frame_to[slot], frame_sends[slot],
            )

    def end_totals(head):
        for slot in range(2):
            arrive(head, TOTAL + slot, total.at[head, 2 * slot], frame_gets[slot])

    def second_pass(head):
        for ff in range(3):
            dqt[head, ff] = jnp.zeros((HS, ROWS), jnp.float32)

        def body(i, carry):
            own = i >= 4
            rr = jnp.where(own, 5 - i, 1 - i // 2)
            side = i % 2
            cc = jnp.where(own, 1, 2 * side)
            keys, values = kv[head, rr, cc, 0], kv[head, rr, cc, 1]
            keys_t = ktr[head, rr, cc]
            place = row_mask(head, rr) * col_mask(head, cc)
            dkey = jnp.zeros((ROWS, HS), jnp.float32)
            dvalue = jnp.zeros((ROWS, HS), jnp.float32)
            for ff in range(3):
                hide = jnp.where(place * frame_mask(head, ff) == 1, 0.0, HIDE)
                shift = total[head, ff, 0:1] + hide
                centre = total[head, ff, 1:2]
                probs = jnp.exp2(dot(keys, qdt[head, ff, 0]) * EXP_SCALE - shift)
                dprobs = dot(values, qdt[head, ff, 1])
                dscore = (probs * (dprobs - centre)).astype(jnp.bfloat16)
                dvalue = dvalue + dot(probs.astype(jnp.bfloat16), qd[head, ff, 1])
                dkey = dkey + dot(dscore, qd[head, ff, 0])
                dqt[head, ff] += dot(keys_t, dscore)
            dkey = dkey * SCALE

            def keep():
                acc[head, rr, 0] = dkey
                acc[head, rr, 1] = dvalue

            def give():
                col_out[head, rr, side, 0] = dkey.astype(jnp.bfloat16)
                col_out[head, rr, side, 1] = dvalue.astype(jnp.bfloat16)
                to_left = side == 0

                def go():
                    remote(
                        head, GCOL + 2 * rr + (1 - side), col_out.at[head, rr, side],
                        col_in.at[head, rr, 1 - side], "tile", tile + 2 * side - 1,
                    ).start()

                pl.when(jnp.logical_or(
                    jnp.logical_and(to_left, has_left),
                    jnp.logical_and(jnp.logical_not(to_left), has_right),
                ))(go)

            pl.when(own)(keep)
            pl.when(jnp.logical_not(own))(give)
            return carry

        lax.fori_loop(0, 6, body, 0)
        for rr in range(2):
            for slot in range(2):
                started.append((
                    col_sends[slot],
                    lambda rr=rr, slot=slot: remote(
                        head, GCOL + 2 * rr + slot, col_out.at[head, rr, 1 - slot],
                        col_in.at[head, rr, slot], "tile", col_to[slot],
                    ).wait_send(),
                ))

    def send_grads(head):
        for slot in range(2):
            arrive(head, GCOL + 2 + slot, col_in.at[head, 1, slot], col_gets[slot])
        for kind in range(2):
            summed = (
                acc[head, 1, kind]
                + col_in[head, 1, 0, kind].astype(jnp.float32)
                + col_in[head, 1, 1, kind].astype(jnp.float32)
            )
            row_out[head, kind] = summed.astype(jnp.bfloat16)
        send(head, GROW, row_out.at[head], row_in.at[head], partner)
        for slot in range(2):
            dq_out[head, slot] = (dqt[head, 2 - 2 * slot] * SCALE).T.astype(jnp.bfloat16)
            send(
                head, GQ + slot, dq_out.at[head, slot], dq_in.at[head, slot],
                frame_to[slot], frame_sends[slot],
            )

    def finish(head):
        lanes = pl.ds(head * HS, HS)
        for slot in range(2):
            arrive(head, GCOL + slot, col_in.at[head, 0, slot], col_gets[slot])
        arrive(head, GROW, row_in.at[head])
        sums = []
        for kind in range(2):
            sums.append(
                acc[head, 0, kind]
                + col_in[head, 0, 0, kind].astype(jnp.float32)
                + col_in[head, 0, 1, kind].astype(jnp.float32)
                + row_in[head, kind].astype(jnp.float32)
            )
        gk_out[0, :, lanes] = pullback(
            k_ref[0, :, lanes].astype(jnp.float32), gain_k[...], sums[0]
        ).astype(jnp.bfloat16)
        gv_out[0, :, lanes] = sums[1].astype(jnp.bfloat16)
        for slot in range(2):
            arrive(head, GQ + slot, dq_in.at[head, slot], frame_gets[slot])
        dquery = (
            (dqt[head, 1] * SCALE).T
            + dq_in[head, 0].astype(jnp.float32)
            + dq_in[head, 1].astype(jnp.float32)
        )
        gq_out[0, :, lanes] = pullback(
            q_ref[0, :, lanes].astype(jnp.float32), gain_q[...], dquery
        ).astype(jnp.bfloat16)

    start_a2a(0)
    gather_first(0)
    start_a2a(1)
    gather_second(0)
    gather_first(1)
    gather_end(0)
    first_pass(0)
    send_parts(0)
    gather_second(1)
    totals(0)
    end_totals(0)
    second_pass(0)
    send_grads(0)
    gather_end(1)
    first_pass(1)
    send_parts(1)
    totals(1)
    end_totals(1)
    second_pass(1)
    send_grads(1)
    finish(0)
    finish(1)
    for cond, wait in started:
        under(cond, wait)


def shards(query, key, value, grad_out, gain_q, gain_k, window):
    half = jax.ShapeDtypeStruct(query.shape, jnp.bfloat16)
    vmem = pl.BlockSpec(memory_space=pltpu.VMEM)
    low, full = jnp.bfloat16, jnp.float32
    return pl.pallas_call(
        kernel,
        out_shape=(half, half, half),
        in_specs=[pl.BlockSpec(memory_space=pltpu.SMEM)] + [vmem] * 6,
        out_specs=(vmem, vmem, vmem),
        scratch_shapes=[
            pltpu.VMEM((2, 2, 3, 2, ROWS, HS), low),
            pltpu.VMEM((2, 3, 2, ROWS, HS), low),
            pltpu.VMEM((2, 3, 2, HS, ROWS), low),
            pltpu.VMEM((2, 2, 3, HS, ROWS), low),
            pltpu.VMEM((2, 2, 2, ROWS, HS), full),
            pltpu.VMEM((2, 3, HS, ROWS), full),
            pltpu.VMEM((2, 3, 8, ROWS), full),
            pltpu.VMEM((2, 2, 8, ROWS), full),
            pltpu.VMEM((2, 3, 8, ROWS), full),
            pltpu.VMEM((2, 2, 2, 2, ROWS, HS), low),
            pltpu.VMEM((2, 2, 2, 2, ROWS, HS), low),
            pltpu.VMEM((2, 2, ROWS, HS), low),
            pltpu.VMEM((2, 2, ROWS, HS), low),
            pltpu.VMEM((2, 2, ROWS, HS), low),
            pltpu.VMEM((2, 2, ROWS, HS), low),
            pltpu.SemaphoreType.DMA((2, COPIES)),
            pltpu.SemaphoreType.DMA((2, COPIES)),
            pltpu.SemaphoreType.DMA((2,)),
        ],
        compiler_params=pltpu.CompilerParams(
            collective_id=0, has_side_effects=True, vmem_limit_bytes=56 * 1024 * 1024
        ),
    )(window, query, key, value, grad_out, gain_q.reshape(1, HS), gain_k.reshape(1, HS))


def solution(mesh):
    placed = (
        P("tile", None, "head"),
        P("tile", None, "head"),
        P("tile", None, "head"),
        P("tile", "head", None),
        P(),
        P(),
        P("head", None),
    )
    return jax.shard_map(
        shards,
        mesh=mesh,
        in_specs=placed,
        out_specs=(P("tile", None, "head"), P("tile", None, "head"), P("tile", None, "head")),
        check_vma=False,
    )
```

time: 907 us -> 83.2 us (0.09)
  the two profiles are of different devices: /device:TPU:1 before, /device:TPU:100 now
where the time goes in v1:
time: 83.2 us; the launch traced here: 83.1 us
  Pallas kernels  79.1 us (95%)
  local copies, waits for them, and re-layouts  3.33 us (4%)
    pallas_call x1, Pallas kernels, shards(): pl.pallas_call(kernel, out_shape=(half, half, half), in_specs=[pl.BlockSp...  79.1 us
    unnamed x7, local copies, waits for them, and re-layouts  3.33 us

profile of v1, /device:TPU:100, one launch (start us, length us, event | category | flops | bytes accessed | tf_op | source)
XLA Modules:
  0.0 83.1 jit_solution(4380722717284882239)
XLA Ops:
  0.6 79.1 %shard_map.94 = (bf16[1,384,256]{2,1,0:T(8,128)(2,1)}, bf16[1,384,256]{2,1,0:T(8,128)(2,1)}, bf16[1,384,256]{2,1,0:T(8,128)(2,1)}) custom-call(s32[2,6]{1,0:T(2,128)} %window.1, bf16[1,384,256]{2,1,0:T(8,128)(2,1)} %q_ref.1, bf16[1,384,256]{2,1,0:T(8,128)(2,1)} %k_ref.1, bf16[1,384,256]{2,1,0:T(8,128)(2,1)} %v_ref.1, bf16[1,48,2048]{2,1,0:T(8,128)(2,1)} %g_ref.1, ...), custom_call_target="tpu_custom_call" | custom-call | tf_op jit(solution)/shard_map/pallas_call | solution.py:413
  79.7 0.0 copy-start.1
  79.7 1.7 %copy.13 = bf16[1,384,256]{2,1,0:T(8,128)(2,1)} copy(bf16[1,384,256]{2,1,0:T(8,128)(2,1)} %get-tuple-element.6) | data formatting | bytes 393216
  81.4 0.0 copy-done.1
  81.4 0.0 copy-start
  81.4 0.7 copy.14
  82.1 0.3 copy-done
  82.4 0.7 copy.15
Async XLA Ops:
  79.7 1.7 %copy-start.1 = (bf16[1,384,256]{2,1,0:T(8,128)(2,1)S(1)}, bf16[1,384,256]{2,1,0:T(8,128)(2,1)}, u32[]{:S(2)}) copy-start(bf16[1,384,256]{2,1,0:T(8,128)(2,1)} %get-tuple-element.7) | copy-start | bytes 589828
  81.4 1.0 %copy-start = (bf16[1,384,256]{2,1,0:T(8,128)(2,1)S(1)}, bf16[1,384,256]{2,1,0:T(8,128)(2,1)}, u32[]{:S(2)}) copy-start(bf16[1,384,256]{2,1,0:T(8,128)(2,1)} %get-tuple-element.8) | copy-start | bytes 589828

commit v2 on v1

v2 whole, which is shorter than its diff:
```python
import math

import jax
import jax.numpy as jnp
from jax import lax
from jax.experimental import pallas as pl
from jax.experimental.pallas import tpu as pltpu
from jax.sharding import PartitionSpec as P

MESH = pl.DeviceIdType.MESH
HS = 128
TF, TR, TC = 4, 2, 4
ROWS = 384
PIECE = 48
GROUP = 8
PLANE = TR * TC
SCALE = 1.0 / math.sqrt(HS)
EXP_SCALE = SCALE * math.log2(math.e)
EPS = 1e-6

A2A = 0
KVROW = 8
KVCOL = 9
QF = 13
DOF = 15
PART = 17
TOTAL = 19
GCOL = 21
GROW = 25
GQ = 26
COPIES = 28


def dot(a, b):
    return jnp.dot(a, b, preferred_element_type=jnp.float32)


def fold8(x):
    return jnp.sum(x.reshape(x.shape[0] // 8, 8, x.shape[1]), axis=0)


def inv_rms(x):
    return lax.rsqrt(jnp.mean(x * x, axis=-1, keepdims=True) + EPS)


def pullback(x, gain, cotangent):
    rs = inv_rms(x)
    scaled = cotangent * gain
    along = jnp.mean(scaled * x, axis=-1, keepdims=True)
    return rs * scaled - x * (rs * rs * rs * along)


def kernel(
    window, q_hbm, k_hbm, v_hbm, g_ref, gain_q, gain_k,
    dq_sum, dk_sum, dv_sum,
    q_ref, k_ref, v_ref,
    kv, qd, qdt, ktr, acc, dqt, part, part_in, total,
    col_out, col_in, row_out, row_in, dq_out, dq_in, unnorm_kept, dprobs_kept,
    ssem, rsem, lsem,
):
    me = lax.axis_index("head")
    tile = lax.axis_index("tile")
    frame = tile // PLANE
    row = tile // TC % TR
    col = tile % TC
    has_prev, has_next = frame > 0, frame < TF - 1
    has_left, has_right = col > 0, col < TC - 1
    partner = tile + TC * (1 - 2 * row)

    has_remote = jnp.where(row == 0, frame, TF - 1 - frame) > 0
    site = (tile - TC * (1 + row), tile + TC * (2 - row))
    has_site = (has_prev, has_next)
    owner = tuple(tile + TC * (3 * row - 2 + j) for j in range(2))
    my_side = 1 - row

    col_to = (tile + 1, tile - 1)
    col_sends = (has_right, has_left)
    col_gets = (has_left, has_right)

    started = []

    def remote(head, index, src, dst, axis, device, got=None):
        return pltpu.make_async_remote_copy(
            src_ref=src,
            dst_ref=dst,
            send_sem=ssem.at[head, index],
            recv_sem=rsem.at[head, index if got is None else got],
            device_id={axis: device},
            device_id_type=MESH,
        )

    def under(cond, fn):
        if cond is None:
            fn()
        else:
            pl.when(cond)(fn)

    def send(head, index, src, dst, device, cond=None, got=None):
        def copy():
            return remote(head, index, src, dst, "tile", device, got)

        under(cond, lambda: copy().start())
        started.append((cond, lambda: copy().wait_send()))

    def arrive(head, index, dst, cond=None):
        under(cond, lambda: remote(head, index, dst, dst, "tile", partner).wait_recv())

    barrier = pltpu.get_barrier_semaphore()

    def greet(axis, device):
        pl.semaphore_signal(barrier, inc=1, device_id={axis: device}, device_id_type=MESH)

    for step in range(1, GROUP):
        greet("head", lax.rem(me + step, GROUP))
    near = (
        (tile - TC, tile >= TC),
        (tile + TC, tile < TF * PLANE - TC),
        (tile - 2 * TC, has_prev),
        (tile + 2 * TC, has_next),
        (tile - 1, has_left),
        (tile + 1, has_right),
    )
    for device, cond in near:
        under(cond, lambda device=device: greet("tile", device))

    loads = [
        pltpu.make_async_copy(src, dst, lsem.at[2 + at])
        for at, (src, dst) in enumerate(((k_hbm, k_ref), (v_hbm, v_ref), (q_hbm, q_ref)))
    ]
    for load in loads:
        load.start()
    for load in loads:
        load.wait()

    for head in range(2):
        lanes = pl.ds(head * HS, HS)
        x = k_ref[0, :, lanes].astype(jnp.float32)
        kv[head, 0, 1, 0] = (x * inv_rms(x) * gain_k[...]).astype(jnp.bfloat16)
        kv[head, 0, 1, 1] = v_ref[0, :, lanes]
        x = q_ref[0, :, lanes].astype(jnp.float32)
        qd[head, 1, 0] = (x * inv_rms(x) * gain_q[...]).astype(jnp.bfloat16)

    def clear(ref):
        ref[...] = jnp.zeros(ref.shape, ref.dtype)

    def no_remote():
        for head in range(2):
            for j in range(2):
                clear(qd.at[head, 2 * j])
                clear(total.at[head, 2 * j])

    pl.when(jnp.logical_not(has_remote))(no_remote)

    for slot in range(2):
        def no_site(slot=slot):
            for head in range(2):
                clear(part_in.at[head, slot])
                clear(dq_in.at[head, slot])

        def no_col(slot=slot):
            for head in range(2):
                for rr in range(2):
                    clear(kv.at[head, rr, 2 * slot])
                    clear(col_in.at[head, rr, slot])

        pl.when(jnp.logical_not(has_site[slot]))(no_site)
        pl.when(jnp.logical_not(col_gets[slot]))(no_col)

    greeted = GROUP - 1
    for _, cond in near:
        greeted = greeted + jnp.where(cond, 1, 0)
    pl.semaphore_wait(barrier, greeted)

    def a2a(head, step):
        to = lax.rem(me + step, GROUP)
        src = g_ref.at[0, :, pl.ds(pl.multiple_of(to * (2 * HS) + head * HS, HS), HS)]
        dst = qd.at[head, 1, 1, pl.ds(pl.multiple_of(me * PIECE, 16), PIECE), :]
        return remote(head, A2A + step, src, dst, "head", to)

    def own_piece(head):
        src = g_ref.at[0, :, pl.ds(pl.multiple_of(me * (2 * HS) + head * HS, HS), HS)]
        dst = qd.at[head, 1, 1, pl.ds(pl.multiple_of(me * PIECE, 16), PIECE), :]
        return pltpu.make_async_copy(src, dst, lsem.at[head])

    def start_a2a(head):
        for step in range(1, GROUP):
            a2a(head, step).start()
            started.append((None, lambda step=step: a2a(head, step).wait_send()))
        own_piece(head).start()

    def end_a2a(head):
        for step in range(1, GROUP):
            come = lax.rem(me + GROUP - step, GROUP)
            dst = qd.at[head, 1, 1, pl.ds(pl.multiple_of(come * PIECE, 16), PIECE), :]
            remote(head, A2A + step, dst, dst, "head", come).wait_recv()
        own_piece(head).wait()

    def kv_row(head):
        send(head, KVROW, kv.at[head, 0, 1], kv.at[head, 1, 1], partner)

    def kv_cols(head, rr):
        for slot in range(2):
            send(
                head, KVCOL + 2 * rr + slot, kv.at[head, rr, 1], kv.at[head, rr, 2 * slot],
                col_to[slot], col_sends[slot],
            )

    def to_sites(head, base, src, dst):
        for side in range(2):
            send(head, base + side, src, dst, site[side], has_site[side], base + row)

    def to_owners(head, base, srcs, dst):
        for j in range(2):
            send(head, base + j, srcs.at[head, j], dst, owner[j], has_remote, base + my_side)

    def frames(head, base, kind):
        to_sites(head, base, qd.at[head, 1, kind], qd.at[head, 2 * row, kind])

    def gather_first(head):
        kv_row(head)
        kv_cols(head, 0)
        frames(head, QF, 0)

    def cotangents(head):
        end_a2a(head)
        frames(head, DOF, 1)

    def forward_row(head):
        arrive(head, KVROW, kv.at[head, 1, 1])
        kv_cols(head, 1)

    def end_cols(head):
        for slot in range(2):
            for rr in range(2):
                arrive(head, KVCOL + 2 * rr + slot, kv.at[head, rr, 2 * slot], col_gets[slot])

    def end_frames(head):
        for j in range(2):
            arrive(head, QF + j, qd.at[head, 2 * j, 0], has_remote)
            arrive(head, DOF + j, qd.at[head, 2 * j, 1], has_remote)

    def one_if(cond):
        return jnp.where(cond, 1, 0)

    def query_mask(head, ff, rr):
        key_row = jnp.where(rr == 0, row, 1 - row)
        offset = key_row - (0, row, 1)[ff]
        rows = jnp.where(offset == 0, 1, jnp.where(offset > 0, window[head, 3], -window[head, 2]))
        if ff == 1:
            return rows
        frames = jnp.where(row == 0, window[head, 1], -window[head, 0])
        return rows * frames * one_if(has_remote)

    def col_mask(head, cc):
        left = -window[head, 4] * one_if(has_left)
        right = window[head, 5] * one_if(has_right)
        return jnp.where(cc == 0, left, jnp.where(cc == 2, right, 1))

    def first_pass(head, ffs):
        for ff in ffs:
            for kind in range(2):
                qdt[head, ff, kind] = qd[head, ff, kind].T

        def body(i, carry):
            rr, cc = i // 3, i % 3
            keys, values = kv[head, rr, cc, 0], kv[head, rr, cc, 1]
            if 1 in ffs:
                ktr[head, rr, cc] = keys.T
            place = col_mask(head, cc)
            out = []
            for at, ff in enumerate(ffs):
                live = jnp.where(place * query_mask(head, ff, rr) == 1, 1.0, 0.0)
                unnorm = jnp.exp2(dot(keys, qdt[head, ff, 0]) * EXP_SCALE)
                dprobs = dot(values, qdt[head, ff, 1])
                unnorm_kept[head, rr, cc, ff] = unnorm.astype(jnp.bfloat16)
                dprobs_kept[head, rr, cc, ff] = dprobs
                out.append(carry[2 * at] + fold8(unnorm) * live)
                out.append(carry[2 * at + 1] + fold8(unnorm * dprobs) * live)
            return tuple(out)

        zero = jnp.zeros((8, ROWS), jnp.float32)
        sums = lax.fori_loop(0, 6, body, (zero,) * (2 * len(ffs)))
        for at, ff in enumerate(ffs):
            for kind in range(2):
                part[head, ff, kind : kind + 1] = jnp.sum(
                    sums[2 * at + kind], axis=0, keepdims=True
                )
            part[head, ff, 2:8] = jnp.zeros((6, ROWS), jnp.float32)

    def send_parts(head):
        for j in range(2):
            send(
                head, PART + j, part.at[head, 2 * j], part_in.at[head, my_side],
                owner[j], has_remote, PART + my_side,
            )

    def totals(head):
        for slot in range(2):
            arrive(head, PART + slot, part_in.at[head, slot], has_site[slot])
        both = part[head, 1, 0:2] + part_in[head, 0, 0:2] + part_in[head, 1, 0:2]
        total[head, 1, 0:1] = 1.0 / both[0:1]
        total[head, 1, 1:2] = both[1:2] / both[0:1]
        total[head, 1, 2:8] = jnp.zeros((6, ROWS), jnp.float32)
        to_sites(head, TOTAL, total.at[head, 1], total.at[head, 2 * row])

    def end_totals(head):
        for j in range(2):
            arrive(head, TOTAL + j, total.at[head, 2 * j], has_remote)

    def key_tile(head, rr, cc):
        keys_t = ktr[head, rr, cc]
        place = col_mask(head, cc)
        dkey = jnp.zeros((ROWS, HS), jnp.float32)
        dvalue = jnp.zeros((ROWS, HS), jnp.float32)
        for ff in range(3):
            live = jnp.where(place * query_mask(head, ff, rr) == 1, 1.0, 0.0)
            share = total[head, ff, 0:1] * live
            centre = total[head, ff, 1:2]
            probs = unnorm_kept[head, rr, cc, ff].astype(jnp.float32) * share
            dscore = (probs * (dprobs_kept[head, rr, cc, ff] - centre)).astype(jnp.bfloat16)
            dvalue = dvalue + dot(probs.astype(jnp.bfloat16), qd[head, ff, 1])
            dkey = dkey + dot(dscore, qd[head, ff, 0])
            dqt[head, ff] += dot(keys_t, dscore)
        return dkey * SCALE, dvalue

    def grads_cols(head):
        for ff in range(3):
            dqt[head, ff] = jnp.zeros((HS, ROWS), jnp.float32)

        def body(i, carry):
            rr = 1 - i // 2
            side = i % 2
            dkey, dvalue = key_tile(head, rr, 2 * side)
            col_out[head, rr, side, 0] = dkey.astype(jnp.bfloat16)
            col_out[head, rr, side, 1] = dvalue.astype(jnp.bfloat16)

            def go():
                remote(
                    head, GCOL + 2 * rr + (1 - side), col_out.at[head, rr, side],
                    col_in.at[head, rr, 1 - side], "tile", tile + 2 * side - 1,
                ).start()

            pl.when(jnp.where(side == 0, one_if(has_left), one_if(has_right)) == 1)(go)
            return carry

        lax.fori_loop(0, 4, body, 0)
        for rr in range(2):
            for slot in range(2):
                started.append((
                    col_sends[slot],
                    lambda rr=rr, slot=slot: remote(
                        head, GCOL + 2 * rr + slot, col_out.at[head, rr, 1 - slot],
                        col_in.at[head, rr, slot], "tile", col_to[slot],
                    ).wait_send(),
                ))

    def grads_own(head, rr):
        acc[head, rr, 0], acc[head, rr, 1] = key_tile(head, rr, 1)

    def send_row(head):
        for slot in range(2):
            arrive(head, GCOL + 2 + slot, col_in.at[head, 1, slot], col_gets[slot])
        for kind in range(2):
            summed = (
                acc[head, 1, kind]
                + col_in[head, 1, 0, kind].astype(jnp.float32)
                + col_in[head, 1, 1, kind].astype(jnp.float32)
            )
            row_out[head, kind] = summed.astype(jnp.bfloat16)
        send(head, GROW, row_out.at[head], row_in.at[head], partner)

    def send_queries(head):
        for j in range(2):
            dq_out[head, j] = (dqt[head, 2 * j] * SCALE).T.astype(jnp.bfloat16)
        to_owners(head, GQ, dq_out, dq_in.at[head, my_side])

    def finish(head):
        lanes = pl.ds(head * HS, HS)
        for slot in range(2):
            arrive(head, GCOL + slot, col_in.at[head, 0, slot], col_gets[slot])
        arrive(head, GROW, row_in.at[head])
        sums = []
        for kind in range(2):
            sums.append(
                acc[head, 0, kind]
                + col_in[head, 0, 0, kind].astype(jnp.float32)
                + col_in[head, 0, 1, kind].astype(jnp.float32)
                + row_in[head, kind].astype(jnp.float32)
            )
        dk_sum[0, :, lanes] = sums[0]
        dv_sum[0, :, lanes] = sums[1].astype(jnp.bfloat16)
        for slot in range(2):
            arrive(head, GQ + slot, dq_in.at[head, slot], has_site[slot])
        dq_sum[0, :, lanes] = (
            (dqt[head, 1] * SCALE).T
            + dq_in[head, 0].astype(jnp.float32)
            + dq_in[head, 1].astype(jnp.float32)
        )

    start_a2a(0)
    gather_first(0)
    start_a2a(1)
    cotangents(0)
    forward_row(0)
    gather_first(1)
    cotangents(1)
    end_cols(0)
    first_pass(0, (1,))
    end_frames(0)
    first_pass(0, (0, 2))
    send_parts(0)
    forward_row(1)
    end_cols(1)
    first_pass(1, (1,))
    totals(0)
    end_frames(1)
    first_pass(1, (0, 2))
    send_parts(1)
    end_totals(0)
    grads_cols(0)
    totals(1)
    grads_own(0, 1)
    send_row(0)
    grads_own(0, 0)
    send_queries(0)
    end_totals(1)
    grads_cols(1)
    grads_own(1, 1)
    send_row(1)
    grads_own(1, 0)
    send_queries(1)
    finish(0)
    finish(1)
    for cond, wait in started:
        under(cond, wait)


def pull_kernel(q_ref, k_ref, dq_ref, dk_ref, dv_ref, gain_q, gain_k, gq_out, gk_out, gv_out):
    for head in range(2):
        lanes = pl.ds(head * HS, HS)
        for x_ref, d_ref, gain, out in (
            (q_ref, dq_ref, gain_q, gq_out),
            (k_ref, dk_ref, gain_k, gk_out),
        ):
            x = x_ref[0, :, lanes].astype(jnp.float32)
            out[0, :, lanes] = pullback(x, gain[...], d_ref[0, :, lanes]).astype(jnp.bfloat16)
    gv_out[...] = dv_ref[...]


def shards(query, key, value, grad_out, gain_q, gain_k, window):
    half = jax.ShapeDtypeStruct(query.shape, jnp.bfloat16)
    wide = jax.ShapeDtypeStruct(query.shape, jnp.float32)
    vmem = pl.BlockSpec(memory_space=pltpu.VMEM)
    anywhere = pl.BlockSpec(memory_space=pl.ANY)
    low, full = jnp.bfloat16, jnp.float32
    gain_q, gain_k = gain_q.reshape(1, HS), gain_k.reshape(1, HS)
    dquery, dkey, dvalue = pl.pallas_call(
        kernel,
        out_shape=(wide, wide, half),
        in_specs=[pl.BlockSpec(memory_space=pltpu.SMEM)] + [anywhere] * 4 + [vmem] * 2,
        out_specs=(vmem, vmem, vmem),
        scratch_shapes=[
            pltpu.VMEM(query.shape, low),
            pltpu.VMEM(query.shape, low),
            pltpu.VMEM(query.shape, low),
            pltpu.VMEM((2, 2, 3, 2, ROWS, HS), low),
            pltpu.VMEM((2, 3, 2, ROWS, HS), low),
            pltpu.VMEM((2, 3, 2, HS, ROWS), low),
            pltpu.VMEM((2, 2, 3, HS, ROWS), low),
            pltpu.VMEM((2, 2, 2, ROWS, HS), full),
            pltpu.VMEM((2, 3, HS, ROWS), full),
            pltpu.VMEM((2, 3, 8, ROWS), full),
            pltpu.VMEM((2, 2, 8, ROWS), full),
            pltpu.VMEM((2, 3, 8, ROWS), full),
            pltpu.VMEM((2, 2, 2, 2, ROWS, HS), low),
            pltpu.VMEM((2, 2, 2, 2, ROWS, HS), low),
            pltpu.VMEM((2, 2, ROWS, HS), low),
            pltpu.VMEM((2, 2, ROWS, HS), low),
            pltpu.VMEM((2, 2, ROWS, HS), low),
            pltpu.VMEM((2, 2, ROWS, HS), low),
            pltpu.VMEM((2, 2, 3, 3, ROWS, ROWS), low),
            pltpu.VMEM((2, 2, 3, 3, ROWS, ROWS), full),
            pltpu.SemaphoreType.DMA((2, COPIES)),
            pltpu.SemaphoreType.DMA((2, COPIES)),
            pltpu.SemaphoreType.DMA((5,)),
        ],
        compiler_params=pltpu.CompilerParams(
            collective_id=0, has_side_effects=True, vmem_limit_bytes=60 * 1024 * 1024
        ),
    )(window, query, key, value, grad_out, gain_q, gain_k)
    return pl.pallas_call(
        pull_kernel,
        out_shape=(half, half, half),
        in_specs=[vmem] * 7,
        out_specs=(vmem, vmem, vmem),
    )(query, key, dquery, dkey, dvalue, gain_q, gain_k)


def solution(mesh):
    placed = (
        P("tile", None, "head"),
        P("tile", None, "head"),
        P("tile", None, "head"),
        P("tile", "head", None),
        P(),
        P(),
        P("head", None),
    )
    return jax.shard_map(
        shards,
        mesh=mesh,
        in_specs=placed,
        out_specs=(P("tile", None, "head"), P("tile", None, "head"), P("tile", None, "head")),
        check_vma=False,
    )
```

time: 83.2 us -> 60.8 us (0.73)
  the two profiles are of different devices: /device:TPU:100 before, /device:TPU:1 now
where the time goes in v2:
time: 60.8 us; the launch traced here: 60.7 us
  Pallas kernels  60 us (99%)
  between operations  0.64 us (1%)
    pallas_call x1, Pallas kernels, shards(): pl.pallas_call(kernel, out_shape=(wide, wide, half), in_specs=[pl.BlockSp...  57.4 us
    pallas_call x1, Pallas kernels, shards(): pl.pallas_call(pull_kernel, out_shape=(half, half, half), in_specs=[vmem]...  2.58 us

profile of v2, /device:TPU:1, one launch (start us, length us, event | category | flops | bytes accessed | tf_op | source)
XLA Modules:
  0.0 60.7 jit_solution(17302817734402965767)
XLA Ops:
  0.6 57.4 %shard_map.94 = (f32[1,384,256]{2,1,0:T(8,128)}, f32[1,384,256]{2,1,0:T(8,128)}, bf16[1,384,256]{2,1,0:T(8,128)(2,1)}) custom-call(s32[2,6]{1,0:T(2,128)} %window.1, bf16[1,384,256]{2,1,0:T(8,128)(2,1)} %q_ref.1, bf16[1,384,256]{2,1,0:T(8,128)(2,1)} %k_ref.1, bf16[1,384,256]{2,1,0:T(8,128)(2,1)} %v_hbm.1, bf16[1,48,2048]{2,1,0:T(8,128)(2,1)} %g_ref.1, ...), custom_call_target="tpu_custom_call" | custom-call | tf_op jit(solution)/shard_map/pallas_call | solution.py:457
  58.1 2.6 %shard_map.95 = (bf16[1,384,256]{2,1,0:T(8,128)(2,1)}, bf16[1,384,256]{2,1,0:T(8,128)(2,1)}, bf16[1,384,256]{2,1,0:T(8,128)(2,1)}) custom-call(bf16[1,384,256]{2,1,0:T(8,128)(2,1)} %q_ref.1, bf16[1,384,256]{2,1,0:T(8,128)(2,1)} %k_ref.1, f32[1,384,256]{2,1,0:T(8,128)} %get-tuple-element.6.dq_ref, f32[1,384,256]{2,1,0:T(8,128)} %get-tuple-element.7.dk_ref, ...), custom_call_target="tpu_custom_call" | custom-call | tf_op jit(solution)/shard_map/pallas_call | solution.py:491

commit v3 on v2

--- a/solution.py
+++ b/solution.py
@@ -24,11 +24,14 @@
 QF = 13
 DOF = 15
 PART = 17
-TOTAL = 19
+OWNPART = 19
 GCOL = 21
 GROW = 25
 GQ = 26
-COPIES = 28
+OPPOSITE = 28
+COPIES = 29
+
+OWN = 2
 
 
 def dot(a, b):
@@ -54,7 +57,7 @@
     window, q_hbm, k_hbm, v_hbm, g_ref, gain_q, gain_k,
     dq_sum, dk_sum, dv_sum,
     q_ref, k_ref, v_ref,
-    kv, qd, qdt, ktr, acc, dqt, part, part_in, total,
+    kv, qd, qdt, ktr, acc, dqt, part, part_in, own_in, opp_in, total,
     col_out, col_in, row_out, row_in, dq_out, dq_in, unnorm_kept, dprobs_kept,
     ssem, rsem, lsem,
 ):
@@ -72,6 +75,8 @@
     has_site = (has_prev, has_next)
     owner = tuple(tile + TC * (3 * row - 2 + j) for j in range(2))
     my_side = 1 - row
+    opposite = tile + 3 * TC * (2 * row - 1)
+    has_opposite = jnp.where(row == 0, frame, TF - 1 - frame) > 1
 
     col_to = (tile + 1, tile - 1)
     col_sends = (has_right, has_left)
@@ -117,6 +122,7 @@
         (tile + TC, tile < TF * PLANE - TC),
         (tile - 2 * TC, has_prev),
         (tile + 2 * TC, has_next),
+        (opposite, has_opposite),
         (tile - 1, has_left),
         (tile + 1, has_right),
     )
@@ -138,18 +144,24 @@
         kv[head, 0, 1, 0] = (x * inv_rms(x) * gain_k[...]).astype(jnp.bfloat16)
         kv[head, 0, 1, 1] = v_ref[0, :, lanes]
         x = q_ref[0, :, lanes].astype(jnp.float32)
-        qd[head, 1, 0] = (x * inv_rms(x) * gain_q[...]).astype(jnp.bfloat16)
+        qd[head, 0, OWN] = (x * inv_rms(x) * gain_q[...]).astype(jnp.bfloat16)
 
     def clear(ref):
         ref[...] = jnp.zeros(ref.shape, ref.dtype)
 
     def no_remote():
         for head in range(2):
-            for j in range(2):
-                clear(qd.at[head, 2 * j])
-                clear(total.at[head, 2 * j])
+            clear(total.at[head])
+            for kind in range(2):
+                clear(qd.at[head, kind, pl.ds(0, 2)])
 
     pl.when(jnp.logical_not(has_remote))(no_remote)
+
+    def no_opposite():
+        for head in range(2):
+            clear(opp_in.at[head])
+
+    pl.when(jnp.logical_not(has_opposite))(no_opposite)
 
     for slot in range(2):
         def no_site(slot=slot):
@@ -174,12 +186,12 @@
     def a2a(head, step):
         to = lax.rem(me + step, GROUP)
         src = g_ref.at[0, :, pl.ds(pl.multiple_of(to * (2 * HS) + head * HS, HS), HS)]
-        dst = qd.at[head, 1, 1, pl.ds(pl.multiple_of(me * PIECE, 16), PIECE), :]
+        dst = qd.at[head, 1, OWN, pl.ds(pl.multiple_of(me * PIECE, 16), PIECE), :]
         return remote(head, A2A + step, src, dst, "head", to)
 
     def own_piece(head):
         src = g_ref.at[0, :, pl.ds(pl.multiple_of(me * (2 * HS) + head * HS, HS), HS)]
-        dst = qd.at[head, 1, 1, pl.ds(pl.multiple_of(me * PIECE, 16), PIECE), :]
+        dst = qd.at[head, 1, OWN, pl.ds(pl.multiple_of(me * PIECE, 16), PIECE), :]
         return pltpu.make_async_copy(src, dst, lsem.at[head])
 
     def start_a2a(head):
@@ -191,7 +203,7 @@
     def end_a2a(head):
         for step in range(1, GROUP):
             come = lax.rem(me + GROUP - step, GROUP)
-            dst = qd.at[head, 1, 1, pl.ds(pl.multiple_of(come * PIECE, 16), PIECE), :]
+            dst = qd.at[head, 1, OWN, pl.ds(pl.multiple_of(come * PIECE, 16), PIECE), :]
             remote(head, A2A + step, dst, dst, "head", come).wait_recv()
         own_piece(head).wait()
 
@@ -214,7 +226,7 @@
             send(head, base + j, srcs.at[head, j], dst, owner[j], has_remote, base + my_side)
 
     def frames(head, base, kind):
-        to_sites(head, base, qd.at[head, 1, kind], qd.at[head, 2 * row, kind])
+        to_sites(head, base, qd.at[head, kind, OWN], qd.at[head, kind, row])
 
     def gather_first(head):
         kv_row(head)
@@ -236,17 +248,17 @@
 
     def end_frames(head):
         for j in range(2):
-            arrive(head, QF + j, qd.at[head, 2 * j, 0], has_remote)
-            arrive(head, DOF + j, qd.at[head, 2 * j, 1], has_remote)
+            arrive(head, QF + j, qd.at[head, 0, j], has_remote)
+            arrive(head, DOF + j, qd.at[head, 1, j], has_remote)
 
     def one_if(cond):
         return jnp.where(cond, 1, 0)
 
     def query_mask(head, ff, rr):
         key_row = jnp.where(rr == 0, row, 1 - row)
-        offset = key_row - (0, row, 1)[ff]
+        offset = key_row - (0, 1, row)[ff]
         rows = jnp.where(offset == 0, 1, jnp.where(offset > 0, window[head, 3], -window[head, 2]))
-        if ff == 1:
+        if ff == OWN:
             return rows
         frames = jnp.where(row == 0, window[head, 1], -window[head, 0])
         return rows * frames * one_if(has_remote)
@@ -256,30 +268,35 @@
         right = window[head, 5] * one_if(has_right)
         return jnp.where(cc == 0, left, jnp.where(cc == 2, right, 1))
 
+    def live(head, rr, cc, ff):
+        return jnp.where(col_mask(head, cc) * query_mask(head, ff, rr) == 1, 1.0, 0.0)
+
     def first_pass(head, ffs):
+        lanes = pl.ds(ffs[0] * ROWS, len(ffs) * ROWS)
         for ff in ffs:
             for kind in range(2):
-                qdt[head, ff, kind] = qd[head, ff, kind].T
+                qdt[head, kind, :, pl.ds(ff * ROWS, ROWS)] = qd[head, kind, ff].T
 
         def body(i, carry):
             rr, cc = i // 3, i % 3
             keys, values = kv[head, rr, cc, 0], kv[head, rr, cc, 1]
-            if 1 in ffs:
+            if OWN in ffs:
                 ktr[head, rr, cc] = keys.T
-            place = col_mask(head, cc)
+            unnorm = jnp.exp2(dot(keys, qdt[head, 0, :, lanes]) * EXP_SCALE)
+            dprobs = dot(values, qdt[head, 1, :, lanes])
+            unnorm_kept[head, rr, cc, :, lanes] = unnorm.astype(jnp.bfloat16)
+            dprobs_kept[head, rr, cc, :, lanes] = dprobs
+            sums = (fold8(unnorm), fold8(unnorm * dprobs))
             out = []
             for at, ff in enumerate(ffs):
-                live = jnp.where(place * query_mask(head, ff, rr) == 1, 1.0, 0.0)
-                unnorm = jnp.exp2(dot(keys, qdt[head, ff, 0]) * EXP_SCALE)
-                dprobs = dot(values, qdt[head, ff, 1])
-                unnorm_kept[head, rr, cc, ff] = unnorm.astype(jnp.bfloat16)
-                dprobs_kept[head, rr, cc, ff] = dprobs
-                out.append(carry[2 * at] + fold8(unnorm) * live)
-                out.append(carry[2 * at + 1] + fold8(unnorm * dprobs) * live)
+                here = live(head, rr, cc, ff)
+                for kind in range(2):
+                    mine = sums[kind][:, at * ROWS : (at + 1) * ROWS]
+                    out.append(carry[2 * at + kind] + mine * here)
             return tuple(out)
 
         zero = jnp.zeros((8, ROWS), jnp.float32)
-        sums = lax.fori_loop(0, 6, body, (zero,) * (2 * len(ffs)))
+        sums = lax.fori_loop(0, 6, body, (zero,) * (2 * len(ffs)), unroll=6)
         for at, ff in enumerate(ffs):
             for kind in range(2):
                 part[head, ff, kind : kind + 1] = jnp.sum(
@@ -287,75 +304,73 @@
                 )
             part[head, ff, 2:8] = jnp.zeros((6, ROWS), jnp.float32)
 
+    def send_own_part(head):
+        to_sites(head, OWNPART, part.at[head, OWN], own_in.at[head, row])
+
     def send_parts(head):
-        for j in range(2):
-            send(
-                head, PART + j, part.at[head, 2 * j], part_in.at[head, my_side],
-                owner[j], has_remote, PART + my_side,
-            )
+        to_owners(head, PART, part, part_in.at[head, my_side])
+        send(
+            head, OPPOSITE, part.at[head, pl.ds(0, 2)], opp_in.at[head], opposite, has_opposite
+        )
 
     def totals(head):
+        def put(ff, terms):
+            both = part[head, ff, 0:2] + terms[0][0:2] + terms[1][0:2]
+            lanes = pl.ds(ff * ROWS, ROWS)
+            total[head, 0:1, lanes] = 1.0 / both[0:1]
+            total[head, 1:2, lanes] = both[1:2] / both[0:1]
+
         for slot in range(2):
             arrive(head, PART + slot, part_in.at[head, slot], has_site[slot])
-        both = part[head, 1, 0:2] + part_in[head, 0, 0:2] + part_in[head, 1, 0:2]
-        total[head, 1, 0:1] = 1.0 / both[0:1]
-        total[head, 1, 1:2] = both[1:2] / both[0:1]
-        total[head, 1, 2:8] = jnp.zeros((6, ROWS), jnp.float32)
-        to_sites(head, TOTAL, total.at[head, 1], total.at[head, 2 * row])
-
-    def end_totals(head):
+        put(OWN, (part_in[head, 0], part_in[head, 1]))
         for j in range(2):
-            arrive(head, TOTAL + j, total.at[head, 2 * j], has_remote)
-
-    def key_tile(head, rr, cc):
-        keys_t = ktr[head, rr, cc]
-        place = col_mask(head, cc)
-        dkey = jnp.zeros((ROWS, HS), jnp.float32)
-        dvalue = jnp.zeros((ROWS, HS), jnp.float32)
-        for ff in range(3):
-            live = jnp.where(place * query_mask(head, ff, rr) == 1, 1.0, 0.0)
-            share = total[head, ff, 0:1] * live
-            centre = total[head, ff, 1:2]
-            probs = unnorm_kept[head, rr, cc, ff].astype(jnp.float32) * share
-            dscore = (probs * (dprobs_kept[head, rr, cc, ff] - centre)).astype(jnp.bfloat16)
-            dvalue = dvalue + dot(probs.astype(jnp.bfloat16), qd[head, ff, 1])
-            dkey = dkey + dot(dscore, qd[head, ff, 0])
-            dqt[head, ff] += dot(keys_t, dscore)
-        return dkey * SCALE, dvalue
-
-    def grads_cols(head):
-        for ff in range(3):
-            dqt[head, ff] = jnp.zeros((HS, ROWS), jnp.float32)
-
-        def body(i, carry):
-            rr = 1 - i // 2
-            side = i % 2
-            dkey, dvalue = key_tile(head, rr, 2 * side)
-            col_out[head, rr, side, 0] = dkey.astype(jnp.bfloat16)
-            col_out[head, rr, side, 1] = dvalue.astype(jnp.bfloat16)
-
-            def go():
-                remote(
-                    head, GCOL + 2 * rr + (1 - side), col_out.at[head, rr, side],
-                    col_in.at[head, rr, 1 - side], "tile", tile + 2 * side - 1,
-                ).start()
-
-            pl.when(jnp.where(side == 0, one_if(has_left), one_if(has_right)) == 1)(go)
-            return carry
-
-        lax.fori_loop(0, 4, body, 0)
-        for rr in range(2):
-            for slot in range(2):
-                started.append((
-                    col_sends[slot],
-                    lambda rr=rr, slot=slot: remote(
-                        head, GCOL + 2 * rr + slot, col_out.at[head, rr, 1 - slot],
-                        col_in.at[head, rr, slot], "tile", col_to[slot],
-                    ).wait_send(),
-                ))
-
-    def grads_own(head, rr):
-        acc[head, rr, 0], acc[head, rr, 1] = key_tile(head, rr, 1)
+            arrive(head, OWNPART + j, own_in.at[head, j], has_remote)
+        arrive(head, OPPOSITE, opp_in.at[head], has_opposite)
+
+        def put_remote():
+            for j in range(2):
+                put(j, (own_in[head, j], opp_in[head, j]))
+
+        pl.when(has_remote)(put_remote)
+
+    def key_tiles(head, places):
+        queries = qd[head, 0].reshape(3 * ROWS, HS)
+        cotangents = qd[head, 1].reshape(3 * ROWS, HS)
+        centre = total[head, 1:2]
+        out, scores = [], []
+        for rr, cc in places:
+            alive = jnp.concatenate(
+                [jnp.full((1, ROWS), live(head, rr, cc, ff), jnp.float32) for ff in range(3)],
+                axis=1,
+            )
+            share = total[head, 0:1] * alive
+            probs = unnorm_kept[head, rr, cc].astype(jnp.float32) * share
+            dscore = (probs * (dprobs_kept[head, rr, cc] - centre)).astype(jnp.bfloat16)
+            dvalue = dot(probs.astype(jnp.bfloat16), cotangents)
+            out.append((dot(dscore, queries) * SCALE, dvalue))
+            scores.append(dscore)
+        keys_t = jnp.concatenate([ktr[head, rr, cc] for rr, cc in places], axis=1)
+        dqt[head] += dot(keys_t, jnp.concatenate(scores, axis=0))
+        return out
+
+    def give_col(head, rr, cc, grads):
+        side = cc // 2
+        for kind in range(2):
+            col_out[head, rr, side, kind] = grads[kind].astype(jnp.bfloat16)
+        slot = 1 - side
+        send(
+            head, GCOL + 2 * rr + slot, col_out.at[head, rr, side], col_in.at[head, rr, slot],
+            col_to[slot], col_sends[slot],
+        )
+
+    def second_pass(head):
+        dqt[head] = jnp.zeros((HS, 3 * ROWS), jnp.float32)
+        for places in (((1, 0), (1, 2)), ((1, 1), (0, 0)), ((0, 2), (0, 1))):
+            for (rr, cc), grads in zip(places, key_tiles(head, places)):
+                if cc == 1:
+                    acc[head, rr, 0], acc[head, rr, 1] = grads
+                else:
+                    give_col(head, rr, cc, grads)
 
     def send_row(head):
         for slot in range(2):
@@ -371,7 +386,7 @@
 
     def send_queries(head):
         for j in range(2):
-            dq_out[head, j] = (dqt[head, 2 * j] * SCALE).T.astype(jnp.bfloat16)
+            dq_out[head, j] = (dqt[head, :, pl.ds(j * ROWS, ROWS)] * SCALE).T.astype(jnp.bfloat16)
         to_owners(head, GQ, dq_out, dq_in.at[head, my_side])
 
     def finish(head):
@@ -392,7 +407,7 @@
         for slot in range(2):
             arrive(head, GQ + slot, dq_in.at[head, slot], has_site[slot])
         dq_sum[0, :, lanes] = (
-            (dqt[head, 1] * SCALE).T
+            (dqt[head, :, pl.ds(OWN * ROWS, ROWS)] * SCALE).T
             + dq_in[head, 0].astype(jnp.float32)
             + dq_in[head, 1].astype(jnp.float32)
         )
@@ -405,30 +420,26 @@
     gather_first(1)
     cotangents(1)
     end_cols(0)
-    first_pass(0, (1,))
+    first_pass(0, (OWN,))
+    send_own_part(0)
     end_frames(0)
-    first_pass(0, (0, 2))
+    first_pass(0, (0, 1))
     send_parts(0)
     forward_row(1)
     end_cols(1)
-    first_pass(1, (1,))
+    first_pass(1, (OWN,))
+    send_own_part(1)
+    end_frames(1)
+    first_pass(1, (0, 1))
+    send_parts(1)
     totals(0)
-    end_frames(1)
-    first_pass(1, (0, 2))
-    send_parts(1)
-    end_totals(0)
-    grads_cols(0)
+    second_pass(0)
+    send_queries(0)
+    send_row(0)
     totals(1)
-    grads_own(0, 1)
-    send_row(0)
-    grads_own(0, 0)
-    send_queries(0)
-    end_totals(1)
-    grads_cols(1)
-    grads_own(1, 1)
+    second_pass(1)
+    send_queries(1)
     send_row(1)
-    grads_own(1, 0)
-    send_queries(1)
     finish(0)
     finish(1)
     for cond, wait in started:
@@ -464,22 +475,24 @@
             pltpu.VMEM(query.shape, low),
             pltpu.VMEM(query.shape, low),
             pltpu.VMEM((2, 2, 3, 2, ROWS, HS), low),
-            pltpu.VMEM((2, 3, 2, ROWS, HS), low),
-            pltpu.VMEM((2, 3, 2, HS, ROWS), low),
+            pltpu.VMEM((2, 2, 3, ROWS, HS), low),
+            pltpu.VMEM((2, 2, HS, 3 * ROWS), low),
             pltpu.VMEM((2, 2, 3, HS, ROWS), low),
             pltpu.VMEM((2, 2, 2, ROWS, HS), full),
-            pltpu.VMEM((2, 3, HS, ROWS), full),
+            pltpu.VMEM((2, HS, 3 * ROWS), full),
             pltpu.VMEM((2, 3, 8, ROWS), full),
             pltpu.VMEM((2, 2, 8, ROWS), full),
-            pltpu.VMEM((2, 3, 8, ROWS), full),
+            pltpu.VMEM((2, 2, 8, ROWS), full),
+            pltpu.VMEM((2, 2, 8, ROWS), full),
+            pltpu.VMEM((2, 8, 3 * ROWS), full),
             pltpu.VMEM((2, 2, 2, 2, ROWS, HS), low),
             pltpu.VMEM((2, 2, 2, 2, ROWS, HS), low),
             pltpu.VMEM((2, 2, ROWS, HS), low),
             pltpu.VMEM((2, 2, ROWS, HS), low),
             pltpu.VMEM((2, 2, ROWS, HS), low),
             pltpu.VMEM((2, 2, ROWS, HS), low),
-            pltpu.VMEM((2, 2, 3, 3, ROWS, ROWS), low),
-            pltpu.VMEM((2, 2, 3, 3, ROWS, ROWS), full),
+            pltpu.VMEM((2, 2, 3, ROWS, 3 * ROWS), low),
+            pltpu.VMEM((2, 2, 3, ROWS, 3 * ROWS), full),
             pltpu.SemaphoreType.DMA((2, COPIES)),
             pltpu.SemaphoreType.DMA((2, COPIES)),
             pltpu.SemaphoreType.DMA((5,)),

time: 60.8 us -> 58.4 us (0.961)
  Pallas kernels: 60 us -> 57.6 us
    pallas_call x1, Pallas kernels: 57.4 us -> 55.1 us  [shards(): pl.pallas_call(kernel, out_shape=(wide, wide, half), in_specs=[pl.BlockSp...]
where the time goes in v3:
time: 58.4 us; the launch traced here: 58.3 us
  Pallas kernels  57.6 us (99%)
  between operations  0.64 us (1%)
    pallas_call x1, Pallas kernels, shards(): pl.pallas_call(kernel, out_shape=(wide, wide, half), in_specs=[pl.BlockSp...  55.1 us
    pallas_call x1, Pallas kernels, shards(): pl.pallas_call(pull_kernel, out_shape=(half, half, half), in_specs=[vmem]...  2.58 us

profile of v3, /device:TPU:1, one launch (start us, length us, event | category | flops | bytes accessed | tf_op | source)
XLA Modules:
  0.0 58.3 jit_solution(4143057075556781223)
XLA Ops:
  0.6 55.1 %shard_map.94 = (f32[1,384,256]{2,1,0:T(8,128)}, f32[1,384,256]{2,1,0:T(8,128)}, bf16[1,384,256]{2,1,0:T(8,128)(2,1)}) custom-call(s32[2,6]{1,0:T(2,128)} %window.1, bf16[1,384,256]{2,1,0:T(8,128)(2,1)} %q_ref.1, bf16[1,384,256]{2,1,0:T(8,128)(2,1)} %k_ref.1, bf16[1,384,256]{2,1,0:T(8,128)(2,1)} %v_hbm.1, bf16[1,48,2048]{2,1,0:T(8,128)(2,1)} %g_ref.1, ...), custom_call_target="tpu_custom_call" | custom-call | tf_op jit(solution)/shard_map/pallas_call | solution.py:468
  55.7 2.6 %shard_map.95 = (bf16[1,384,256]{2,1,0:T(8,128)(2,1)}, bf16[1,384,256]{2,1,0:T(8,128)(2,1)}, bf16[1,384,256]{2,1,0:T(8,128)(2,1)}) custom-call(bf16[1,384,256]{2,1,0:T(8,128)(2,1)} %q_ref.1, bf16[1,384,256]{2,1,0:T(8,128)(2,1)} %k_ref.1, f32[1,384,256]{2,1,0:T(8,128)} %get-tuple-element.6.dq_ref, f32[1,384,256]{2,1,0:T(8,128)} %get-tuple-element.7.dk_ref, ...), custom_call_target="tpu_custom_call" | custom-call | tf_op jit(solution)/shard_map/pallas_call | solution.py:504

commit v4 on v3

--- a/solution.py
+++ b/solution.py
@@ -302,7 +302,6 @@
                 part[head, ff, kind : kind + 1] = jnp.sum(
                     sums[2 * at + kind], axis=0, keepdims=True
                 )
-            part[head, ff, 2:8] = jnp.zeros((6, ROWS), jnp.float32)
 
     def send_own_part(head):
         to_sites(head, OWNPART, part.at[head, OWN], own_in.at[head, row])
@@ -315,7 +314,7 @@
 
     def totals(head):
         def put(ff, terms):
-            both = part[head, ff, 0:2] + terms[0][0:2] + terms[1][0:2]
+            both = part[head, ff] + terms[0] + terms[1]
             lanes = pl.ds(ff * ROWS, ROWS)
             total[head, 0:1, lanes] = 1.0 / both[0:1]
             total[head, 1:2, lanes] = both[1:2] / both[0:1]
@@ -415,9 +414,11 @@
     start_a2a(0)
     gather_first(0)
     start_a2a(1)
+    frames(1, QF, 0)
     cotangents(0)
     forward_row(0)
-    gather_first(1)
+    kv_row(1)
+    kv_cols(1, 0)
     cotangents(1)
     end_cols(0)
     first_pass(0, (OWN,))
@@ -480,10 +481,10 @@
             pltpu.VMEM((2, 2, 3, HS, ROWS), low),
             pltpu.VMEM((2, 2, 2, ROWS, HS), full),
             pltpu.VMEM((2, HS, 3 * ROWS), full),
-            pltpu.VMEM((2, 3, 8, ROWS), full),
-            pltpu.VMEM((2, 2, 8, ROWS), full),
-            pltpu.VMEM((2, 2, 8, ROWS), full),
-            pltpu.VMEM((2, 2, 8, ROWS), full),
+            pltpu.VMEM((2, 3, 2, ROWS), full),
+            pltpu.VMEM((2, 2, 2, ROWS), full),
+            pltpu.VMEM((2, 2, 2, ROWS), full),
+            pltpu.VMEM((2, 2, 2, ROWS), full),
             pltpu.VMEM((2, 8, 3 * ROWS), full),
             pltpu.VMEM((2, 2, 2, 2, ROWS, HS), low),
             pltpu.VMEM((2, 2, 2, 2, ROWS, HS), low),

time: 58.4 us -> 57 us (0.976)
  Pallas kernels: 57.6 us -> 56.3 us
    pallas_call x1, Pallas kernels: 55.1 us -> 53.7 us  [shards(): pl.pallas_call(kernel, out_shape=(wide, wide, half), in_specs=[pl.BlockSp...]
where the time goes in v4:
time: 57 us; the launch traced here: 56.9 us
  Pallas kernels  56.3 us (99%)
  between operations  0.64 us (1%)
    pallas_call x1, Pallas kernels, shards(): pl.pallas_call(kernel, out_shape=(wide, wide, half), in_specs=[pl.BlockSp...  53.7 us
    pallas_call x1, Pallas kernels, shards(): pl.pallas_call(pull_kernel, out_shape=(half, half, half), in_specs=[vmem]...  2.58 us

profile of v4, /device:TPU:1, one launch (start us, length us, event | category | flops | bytes accessed | tf_op | source)
XLA Modules:
  0.0 56.9 jit_solution(17487244667411303383)
XLA Ops:
  0.6 53.7 %shard_map.94 = (f32[1,384,256]{2,1,0:T(8,128)}, f32[1,384,256]{2,1,0:T(8,128)}, bf16[1,384,256]{2,1,0:T(8,128)(2,1)}) custom-call(s32[2,6]{1,0:T(2,128)} %window.1, bf16[1,384,256]{2,1,0:T(8,128)(2,1)} %q_ref.1, bf16[1,384,256]{2,1,0:T(8,128)(2,1)} %k_ref.1, bf16[1,384,256]{2,1,0:T(8,128)(2,1)} %v_hbm.1, bf16[1,48,2048]{2,1,0:T(8,128)(2,1)} %g_ref.1, ...), custom_call_target="tpu_custom_call" | custom-call | tf_op jit(solution)/shard_map/pallas_call | solution.py:469
  54.3 2.6 %shard_map.95 = (bf16[1,384,256]{2,1,0:T(8,128)(2,1)}, bf16[1,384,256]{2,1,0:T(8,128)(2,1)}, bf16[1,384,256]{2,1,0:T(8,128)(2,1)}) custom-call(bf16[1,384,256]{2,1,0:T(8,128)(2,1)} %q_ref.1, bf16[1,384,256]{2,1,0:T(8,128)(2,1)} %k_ref.1, f32[1,384,256]{2,1,0:T(8,128)} %get-tuple-element.6.dq_ref, f32[1,384,256]{2,1,0:T(8,128)} %get-tuple-element.7.dk_ref, ...), custom_call_target="tpu_custom_call" | custom-call | tf_op jit(solution)/shard_map/pallas_call | solution.py:505

commit v5 on v4

--- a/solution.py
+++ b/solution.py
@@ -230,8 +230,8 @@
 
     def gather_first(head):
         kv_row(head)
+        frames(head, QF, 0)
         kv_cols(head, 0)
-        frames(head, QF, 0)
 
     def cotangents(head):
         end_a2a(head)
@@ -418,8 +418,8 @@
     cotangents(0)
     forward_row(0)
     kv_row(1)
+    cotangents(1)
     kv_cols(1, 0)
-    cotangents(1)
     end_cols(0)
     first_pass(0, (OWN,))
     send_own_part(0)
@@ -438,12 +438,15 @@
     send_queries(0)
     send_row(0)
     totals(1)
+    before = len(started)
     second_pass(1)
     send_queries(1)
     send_row(1)
+    for cond, wait in started[:before]:
+        under(cond, wait)
     finish(0)
     finish(1)
-    for cond, wait in started:
+    for cond, wait in started[before:]:
         under(cond, wait)
 
 

time: 57 us -> 57 us (level)
  no operation moved by 1% of the time
where the time goes in v5:
time: 57 us; the launch traced here: 56.8 us
  Pallas kernels  56.2 us (99%)
  between operations  0.64 us (1%)
    pallas_call x1, Pallas kernels, shards(): pl.pallas_call(kernel, out_shape=(wide, wide, half), in_specs=[pl.BlockSp...  53.6 us
    pallas_call x1, Pallas kernels, shards(): pl.pallas_call(pull_kernel, out_shape=(half, half, half), in_specs=[vmem]...  2.58 us

profile of v5, /device:TPU:1, one launch (start us, length us, event | category | flops | bytes accessed | tf_op | source)
XLA Modules:
  0.0 56.8 jit_solution(6538980961359134466)
XLA Ops:
  0.6 53.6 %shard_map.94 = (f32[1,384,256]{2,1,0:T(8,128)}, f32[1,384,256]{2,1,0:T(8,128)}, bf16[1,384,256]{2,1,0:T(8,128)(2,1)}) custom-call(s32[2,6]{1,0:T(2,128)} %window.1, bf16[1,384,256]{2,1,0:T(8,128)(2,1)} %q_ref.1, bf16[1,384,256]{2,1,0:T(8,128)(2,1)} %k_ref.1, bf16[1,384,256]{2,1,0:T(8,128)(2,1)} %v_hbm.1, bf16[1,48,2048]{2,1,0:T(8,128)(2,1)} %g_ref.1, ...), custom_call_target="tpu_custom_call" | custom-call | tf_op jit(solution)/shard_map/pallas_call | solution.py:472
  54.2 2.6 %shard_map.95 = (bf16[1,384,256]{2,1,0:T(8,128)(2,1)}, bf16[1,384,256]{2,1,0:T(8,128)(2,1)}, bf16[1,384,256]{2,1,0:T(8,128)(2,1)}) custom-call(bf16[1,384,256]{2,1,0:T(8,128)(2,1)} %q_ref.1, bf16[1,384,256]{2,1,0:T(8,128)(2,1)} %k_ref.1, f32[1,384,256]{2,1,0:T(8,128)} %get-tuple-element.6.dq_ref, f32[1,384,256]{2,1,0:T(8,128)} %get-tuple-element.7.dk_ref, ...), custom_call_target="tpu_custom_call" | custom-call | tf_op jit(solution)/shard_map/pallas_call | solution.py:508
